TPU v7x, 128 devices: a whole 4x4x4 slice. The times are simulated.
128 devices in a mesh: fsdp: 32 (over z, y, core), rep: 4 (over x).
Axes of the slice: x: 4, y: 4, z: 4, core: 2. Of those that a mesh axis runs over, the one named last changes fastest.
Arguments:
- tokens: bfloat16 [16384, 2048], P(('fsdp', 'rep')), may hold values from -6 to 6
- cotangent: bfloat16 [16384, 2048], P(('fsdp', 'rep')), may hold values from -6 to 6
- lengths: int32 [128], P(('fsdp', 'rep')), may hold values from 26 to 128, as said below
- qkv_weight: float32 [2048, 2560], P('fsdp'), may hold values from -0.125 to 0.125
- qkv_moment: float32 [2048, 2560], P('fsdp'), may hold values from -32 to 32
- qkv_second: float32 [2048, 2560], P('fsdp'), may hold values from 2.7306666 to 10.922667
- out_weight: float32 [2048, 2048], P('fsdp'), may hold values from -0.25 to 0.25
- out_moment: float32 [2048, 2048], P('fsdp'), may hold values from -20 to 20
- out_second: float32 [2048, 2048], P('fsdp'), may hold values from 0.98304 to 3.93216
- gateup_weight: float32 [2048, 11264], P('fsdp'), may hold values from -0.125 to 0.125
- gateup_moment: float32 [2048, 11264], P('fsdp'), may hold values from -20 to 20
- gateup_second: float32 [2048, 11264], P('fsdp'), may hold values from 0.98304 to 3.93216
- down_weight: float32 [5632, 2048], P('fsdp'), may hold values from -0.078125 to 0.078125
- down_moment: float32 [5632, 2048], P('fsdp'), may hold values from -32 to 32
- down_second: float32 [5632, 2048], P('fsdp'), may hold values from 2.7306666 to 10.922667
- gains: float32 [2, 2048], replicated, may hold values from 0.5 to 1.5
- gain_moment: float32 [2, 2048], replicated, may hold values from -40 to 40
- gain_second: float32 [2, 2048], replicated, may hold values from 3.93216 to 15.72864
Outputs:
- block_output: bfloat16 [16384, 2048], P(('fsdp', 'rep'))
- input_grad: float32 [16384, 2048], P(('fsdp', 'rep'))
- qkv_moment_new: float32 [2048, 2560], P('fsdp')
- qkv_second_new: float32 [2048, 2560], P('fsdp')
- qkv_weight_new: float32 [2048, 2560], P('fsdp')
- out_moment_new: float32 [2048, 2048], P('fsdp')
- out_second_new: float32 [2048, 2048], P('fsdp')
- out_weight_new: float32 [2048, 2048], P('fsdp')
- gateup_moment_new: float32 [2048, 11264], P('fsdp')
- gateup_second_new: float32 [2048, 11264], P('fsdp')
- gateup_weight_new: float32 [2048, 11264], P('fsdp')
- down_moment_new: float32 [5632, 2048], P('fsdp')
- down_second_new: float32 [5632, 2048], P('fsdp')
- down_weight_new: float32 [5632, 2048], P('fsdp')
- gain_moment_new: float32 [2, 2048], replicated
- gain_second_new: float32 [2, 2048], replicated
- gains_new: float32 [2, 2048], replicated
Inputs may be any that keep to these rules, and one draw needn't show every extreme that they name: `lengths`: each device's slots hold one sequence from slot 0; the rest are padding. the last sequence fills all 128 slots.
All inputs are finite; a program needn't handle non-finite values.
Results may differ from a plain program's by a relative error of at most 0.025.
Values may be sent and summed in bfloat16 or wider, within the bound.
No kernel may reach another device: no remote copies, remote signals or barrier semaphores. Data moves between devices by JAX's collectives and lax.ppermute only.
A program may use at most 448 MiB of HBM per device.

v0:
```python
import jax
import jax.numpy as jnp
from jax import lax
from jax.sharding import Mesh
from jax.sharding import PartitionSpec as P

QUERY_HEADS = 32
KEY_VALUE_HEADS = 4
HEAD_SIZE = 64
FF = 5632
STEP = 10
FSDP = ("fsdp_0", "fsdp_1", "fsdp_2")
FSDP_REP = ("fsdp_0", "fsdp_1", "fsdp_2", "rep")


norm_epsilon = 1e-05
beta_one = 0.9
beta_two = 0.999
adam_epsilon = 1e-08
matrix_rate = 0.02
matrix_decay = 0.1
gain_rate = 0.5
masked_score = -1e30


def in_one_piece(arrays, axis, dim, along):
    both = jnp.concatenate(arrays, axis=along)
    out, at, done = (lax.all_gather(both, axis, axis=dim, tiled=True), 0, [])
    for a in arrays:
        done.append(lax.slice_in_dim(out, at, at + a.shape[along], axis=along))
        at += a.shape[along]
    return tuple(done)


def reduce_rows(term_fn, shard_rows):
    summed = lax.psum_scatter(
        term_fn(jnp.int32(0), shard_rows * lax.axis_size(FSDP)).astype(jnp.bfloat16),
        FSDP,
        scatter_dimension=0,
        tiled=True,
    ).astype(jnp.float32)
    return summed


def apply_forward(whole, source):
    return jnp.dot(source, whole, preferred_element_type=jnp.float32)


def apply_backward(whole, source):
    return lax.dot_general(
        source, whole, (((1,), (1,)), ((), ())), preferred_element_type=jnp.float32
    )


def weight_terms(source, grads):

    def term_fn(start, token_count):
        return lax.dot_general(
            source, grads, (((0,), (0,)), ((), ())), preferred_element_type=jnp.float32
        )

    return term_fn


def norm_forward(values, gain):
    inverse = lax.rsqrt(jnp.mean(values * values, axis=-1, keepdims=True) + norm_epsilon)
    return (values * inverse * gain, inverse)


def norm_backward(values, inverse, gain, grads):
    scaled = grads * gain
    gain_grad = jnp.sum(grads * values * inverse, axis=0)
    value_grad = inverse * scaled - values * (inverse * inverse * inverse) * jnp.mean(
        scaled * values, axis=-1, keepdims=True
    )
    return (value_grad, gain_grad)


def rotary_tables(token_count):
    positions = jnp.arange(token_count, dtype=jnp.float32)
    exponents = jnp.arange(0, HEAD_SIZE, 2, dtype=jnp.float32) / HEAD_SIZE
    freqs = jnp.power(10000.0, -exponents)
    angles = positions[:, None] * freqs[None, :]
    angles = jnp.concatenate([angles, angles], axis=-1)[:, None, :]
    return (jnp.cos(angles), jnp.sin(angles))


def rotate_pairs(values, cosine_table, sine_table):
    half = values.shape[-1] // 2
    turned = jnp.concatenate([-values[..., half:], values[..., :half]], axis=-1)
    return values * cosine_table + turned * sine_table


def unrotate(values, cosine_table, sine_table):
    half = values.shape[-1] // 2
    product = values * sine_table
    turned = jnp.concatenate([product[..., half:], -product[..., :half]], axis=-1)
    return values * cosine_table + turned


def causal_scores(query_rows, key):
    token_count = query_rows.shape[0]
    scores = jnp.einsum(
        "tgd,sd->gts", query_rows, key, preferred_element_type=jnp.float32
    ) * HEAD_SIZE ** (-0.5)
    row_index = lax.broadcasted_iota(jnp.int32, (token_count, token_count), 0)
    col_index = lax.broadcasted_iota(jnp.int32, (token_count, token_count), 1)
    return jnp.where(row_index >= col_index, scores, masked_score)


def head_forward(parts):
    query_rows, key, value_rows = parts
    scores = causal_scores(query_rows, key)
    top = jnp.max(scores, axis=-1, keepdims=True)
    expos = jnp.exp(scores - top)
    totals = jnp.sum(expos, axis=-1, keepdims=True)
    probs = (expos / totals).astype(jnp.bfloat16)
    mixed = jnp.einsum("gts,sd->tgd", probs, value_rows, preferred_element_type=jnp.float32)
    return (mixed, top + jnp.log(totals))


def head_backward(parts):
    query_rows, key, value_rows, grads, logsum = parts
    scores = causal_scores(query_rows, key)
    probs = jnp.exp(scores - logsum)
    value_grad = jnp.einsum(
        "gts,tgd->sd", probs.astype(jnp.bfloat16), grads, preferred_element_type=jnp.float32
    )
    prob_grad = jnp.einsum("tgd,sd->gts", grads, value_rows, preferred_element_type=jnp.float32)
    delta = jnp.sum(prob_grad * probs, axis=-1, keepdims=True)
    score_grad = (probs * (prob_grad - delta) * HEAD_SIZE ** (-0.5)).astype(jnp.bfloat16)
    query_grad = jnp.einsum("gts,sd->tgd", score_grad, key, preferred_element_type=jnp.float32)
    key_grad = jnp.einsum("gts,tgd->sd", score_grad, query_rows, preferred_element_type=jnp.float32)
    return (query_grad, key_grad, value_grad)


def adamw(weight, grad, moment, second, rate, decay):
    moment = beta_one * moment + (1.0 - beta_one) * grad
    second = beta_two * second + (1.0 - beta_two) * grad * grad
    fix_one = 1.0 - beta_one**STEP
    fix_two = 1.0 - beta_two**STEP
    weight = weight - rate * (
        moment / fix_one / (jnp.sqrt(second / fix_two) + adam_epsilon) + decay * weight
    )
    return (moment, second, weight)


def body(
    tokens,
    cotangent,
    lengths,
    qkv_weight,
    qkv_moment,
    qkv_second,
    out_weight,
    out_moment,
    out_second,
    gateup_weight,
    gateup_moment,
    gateup_second,
    down_weight,
    down_moment,
    down_second,
    gains,
    gain_moment,
    gain_second,
):
    token_count = tokens.shape[0]
    head_group = QUERY_HEADS // KEY_VALUE_HEADS
    model_width = QUERY_HEADS * HEAD_SIZE
    key_value_width = KEY_VALUE_HEADS * HEAD_SIZE
    inputs = tokens.astype(jnp.float32)
    positions = jnp.arange(token_count, dtype=jnp.int32)
    valid = (positions < lengths[0]).astype(jnp.float32)[:, None]
    cosine_table, sine_table = rotary_tables(token_count)
    qkv_low = qkv_weight.astype(jnp.bfloat16)
    out_low = out_weight.astype(jnp.bfloat16)
    gateup_low = gateup_weight.astype(jnp.bfloat16)
    down_low = down_weight.astype(jnp.bfloat16)
    qkv_whole, out_whole, gateup_whole, down_whole = (
        *in_one_piece((qkv_low, out_low, gateup_low), FSDP, 0, 1),
        lax.all_gather(down_low, FSDP, axis=0, tiled=True),
    )
    normed, first_inverse = norm_forward(inputs, gains[0])
    first_low = normed.astype(jnp.bfloat16)
    joined_rows = apply_forward(qkv_whole, first_low)
    query_rows = rotate_pairs(
        joined_rows[:, :model_width].reshape(token_count, QUERY_HEADS, HEAD_SIZE),
        cosine_table,
        sine_table,
    ).astype(jnp.bfloat16)
    key = rotate_pairs(
        joined_rows[:, model_width : model_width + key_value_width].reshape(
            token_count, KEY_VALUE_HEADS, HEAD_SIZE
        ),
        cosine_table,
        sine_table,
    ).astype(jnp.bfloat16)
    value_rows = (
        joined_rows[:, model_width + key_value_width :]
        .reshape(token_count, KEY_VALUE_HEADS, HEAD_SIZE)
        .astype(jnp.bfloat16)
    )
    query_head_rows = jnp.moveaxis(
        query_rows.reshape(token_count, KEY_VALUE_HEADS, head_group, HEAD_SIZE), 1, 0
    )
    key_heads = jnp.moveaxis(key, 1, 0)
    value_heads = jnp.moveaxis(value_rows, 1, 0)
    mixed_heads, logsum = lax.map(head_forward, (query_head_rows, key_heads, value_heads))
    mixed_low = (
        jnp.moveaxis(mixed_heads, 0, 1).reshape(token_count, model_width).astype(jnp.bfloat16)
    )
    branch = apply_forward(out_whole, mixed_low)
    middle = inputs + branch
    second, second_inverse = norm_forward(middle, gains[1])
    second_low = second.astype(jnp.bfloat16)
    both = apply_forward(gateup_whole, second_low)
    gate = both[:, :FF]
    up_part = both[:, FF:]
    hidden_low = (jax.nn.silu(gate) * up_part).astype(jnp.bfloat16)
    output = apply_forward(down_whole, hidden_low)
    block_output = ((middle + output) * valid).astype(jnp.bfloat16)
    result_grad = cotangent.astype(jnp.float32) * valid
    output_low = result_grad.astype(jnp.bfloat16)
    down_grad = reduce_rows(weight_terms(hidden_low, output_low), down_weight.shape[0])
    hidden_grad = apply_backward(down_whole, output_low)
    sigma = jax.nn.sigmoid(gate)
    gate_grad = hidden_grad * up_part * sigma * (1.0 + gate * (1.0 - sigma))
    up_grad = hidden_grad * jax.nn.silu(gate)
    both_grad = jnp.concatenate([gate_grad, up_grad], axis=1).astype(jnp.bfloat16)
    gateup_grad = reduce_rows(weight_terms(second_low, both_grad), gateup_weight.shape[0])
    second_grad = apply_backward(gateup_whole, both_grad)
    middle_extra, second_gain_grad = norm_backward(middle, second_inverse, gains[1], second_grad)
    middle_grad = result_grad + middle_extra
    branch_low = middle_grad.astype(jnp.bfloat16)
    out_grad = reduce_rows(weight_terms(mixed_low, branch_low), out_weight.shape[0])
    mixed_gradient = apply_backward(out_whole, branch_low).astype(jnp.bfloat16)
    mixed_gradient_heads = jnp.moveaxis(
        mixed_gradient.reshape(token_count, KEY_VALUE_HEADS, head_group, HEAD_SIZE), 1, 0
    )
    query_grad, key_grad, value_grad = lax.map(
        head_backward, (query_head_rows, key_heads, value_heads, mixed_gradient_heads, logsum)
    )
    query_grad = unrotate(
        jnp.moveaxis(query_grad, 0, 1).reshape(token_count, QUERY_HEADS, HEAD_SIZE),
        cosine_table,
        sine_table,
    )
    key_grad = unrotate(jnp.moveaxis(key_grad, 0, 1), cosine_table, sine_table)
    value_grad = jnp.moveaxis(value_grad, 0, 1)
    joined_grad = jnp.concatenate(
        [
            query_grad.reshape(token_count, model_width),
            key_grad.reshape(token_count, key_value_width),
            value_grad.reshape(token_count, key_value_width),
        ],
        axis=1,
    ).astype(jnp.bfloat16)
    qkv_grad = reduce_rows(weight_terms(first_low, joined_grad), qkv_weight.shape[0])
    first_grad = apply_backward(qkv_whole, joined_grad)
    inputs_extra, first_gain_grad = norm_backward(inputs, first_inverse, gains[0], first_grad)
    input_grad = middle_grad + inputs_extra
    gain_grad = lax.psum(jnp.stack([first_gain_grad, second_gain_grad]), FSDP_REP)
    qkv_total, out_total, gateup_total, down_total = (
        lax.psum(qkv_grad.astype(jnp.bfloat16), "rep").astype(jnp.float32),
        lax.psum(out_grad.astype(jnp.bfloat16), "rep").astype(jnp.float32),
        lax.psum(gateup_grad.astype(jnp.bfloat16), "rep").astype(jnp.float32),
        lax.psum(down_grad.astype(jnp.bfloat16), "rep").astype(jnp.float32),
    )
    qkv_new = adamw(qkv_weight, qkv_total, qkv_moment, qkv_second, matrix_rate, matrix_decay)
    out_new = adamw(out_weight, out_total, out_moment, out_second, matrix_rate, matrix_decay)
    gateup_new = adamw(
        gateup_weight, gateup_total, gateup_moment, gateup_second, matrix_rate, matrix_decay
    )
    down_new = adamw(down_weight, down_total, down_moment, down_second, matrix_rate, matrix_decay)
    gain_new = adamw(gains, gain_grad, gain_moment, gain_second, gain_rate, 0.0)
    return (
        block_output,
        input_grad,
        qkv_new[0],
        qkv_new[1],
        qkv_new[2],
        out_new[0],
        out_new[1],
        out_new[2],
        gateup_new[0],
        gateup_new[1],
        gateup_new[2],
        down_new[0],
        down_new[1],
        down_new[2],
        gain_new[0],
        gain_new[1],
        gain_new[2],
    )


def solution(mesh):
    finer = Mesh(
        mesh.devices.reshape(4, 4, 2, mesh.shape["rep"]), ("fsdp_0", "fsdp_1", "fsdp_2", "rep")
    )
    placed = (
        P(FSDP_REP, None),
        P(FSDP_REP, None),
        P(FSDP_REP),
        P(FSDP, None),
        P(FSDP, None),
        P(FSDP, None),
        P(FSDP, None),
        P(FSDP, None),
        P(FSDP, None),
        P(FSDP, None),
        P(FSDP, None),
        P(FSDP, None),
        P(FSDP, None),
        P(FSDP, None),
        P(FSDP, None),
        P(),
        P(),
        P(),
    )
    return jax.shard_map(
        body,
        mesh=finer,
        in_specs=placed,
        out_specs=(
            P(FSDP_REP, None),
            P(FSDP_REP, None),
            P(FSDP, None),
            P(FSDP, None),
            P(FSDP, None),
            P(FSDP, None),
            P(FSDP, None),
            P(FSDP, None),
            P(FSDP, None),
            P(FSDP, None),
            P(FSDP, None),
            P(FSDP, None),
            P(FSDP, None),
            P(FSDP, None),
            P(),
            P(),
            P(),
        ),
        check_vma=False,
    )
```

profile of v0, /device:TPU:96, one launch (start us, length us, event | category | flops | bytes accessed | tf_op | source)
XLA Modules:
  0.0 976.5 jit_solution(6998494289845735119)
XLA Ops:
  7.3 2.0 convert_element_type.113
  9.4 1.4 pad_maximum_fusion.1
  11.5 1.0 convert_element_type.122
  14.7 191.8 %all-gather.3.cloned.1.call-done = bf16[2048,15872]{1,0:T(8,128)(2,1)} async-done(((bf16[64,15872]{1,0:T(8,128)(2,1)}), bf16[2048,15872]{1,0:T(8,128)(2,1)}) %all-gather.3.cloned.1.call-update) | async-done | bytes 65011728 | tf_op jit(solution)/shard_map/all_gather | solution.py:28
  206.5 5.0 fusion.62
  212.3 1.0 fusion.99
  213.3 8.6 while.28
  213.3 1.2 fusion.174
  215.4 1.2 fusion.174
  217.6 1.2 fusion.174
  219.7 1.2 fusion.174
  221.9 4.9 multiply_reduce_fusion.3
  226.9 19.7 %fusion.58 = f32[128,11264]{1,0:T(8,128)} fusion(bf16[2048,15872]{1,0:T(8,128)(2,1)} %all-gather.3.cloned.1.call-done, f32[128,2048]{1,0:T(8,128)S(1)} %get-tuple-element.179, f32[2048]{0:T(1024)S(1)} %bitcast.191, f32[128]{0:T(128)S(1)} %get-tuple-element.177), kind=kOutput, calls=%fused_computation.71 | convolution fusion | flops 5906366464 | bytes 52961792 | tf_op jit(solution)/shard_map/dot_general | solution.py:46
  246.6 49.9 %all-gather.5.cloned.1.call-done = bf16[5632,2048]{1,0:T(8,128)(2,1)} async-done(((bf16[176,2048]{1,0:T(8,128)(2,1)}), bf16[5632,2048]{1,0:T(8,128)(2,1)}) %all-gather.5.cloned.1.call-update) | async-done | bytes 23068688 | tf_op jit(solution)/shard_map/all_gather | solution.py:182
  296.5 14.7 %multiply_convert_fusion.1 = (bf16[128,5632]{1,0:T(8,128)(2,1)}, bf16[128,5632]{1,0:T(8,128)(2,1)}, bf16[128,5632]{1,0:T(8,128)(2,1)}) fusion(f32[128,11264]{1,0:T(8,128)} %fusion.58, bf16[5632,2048]{1,0:T(8,128)(2,1)} %all-gather.5.cloned.1.call-done, bf16[128,2048]{1,0:T(8,128)(2,1)S(1)} %copy-done.12, f32[128]{0:T(128)S(1)} %copy-done.27), kind=kOutput, calls=%fused_computation.91 | convolution fusion | flops 2964389888 | bytes 33686016 | tf_op jit(solution)/shard_map/dot_general | solution.py:50
  311.3 23.1 %multiply_reduce_fusion.1 = (f32[2048]{0:T(1024)}, f32[128]{0:T(128)S(1)}, f32[128,2048]{1,0:T(8,128)}) fusion(f32[128,2048]{1,0:T(8,128)S(1)} %get-tuple-element.179, f32[128]{0:T(128)S(1)} %get-tuple-element.177, f32[2048]{0:T(1024)S(1)} %bitcast.192, bf16[2048,15872]{1,0:T(8,128)(2,1)} %all-gather.3.cloned.1.call-done, ...), kind=kOutput, calls=%fused_computation.128 | convolution fusion | flops 5912918016 | bytes 51135488 | tf_op jit(solution)/shard_map/dot_general | solution.py:50
  334.4 1.7 subtract_add_fusion
  336.1 5.6 convolution_convert_fusion.3
  341.8 6.3 fusion.75
  348.0 1.0 copy.55
  349.0 28.0 %while.29 = (s32[]{:T(128)}, f32[4,128,8,64]{1,3,2,0:T(8,128)}, f32[4,128,64]{1,2,0:T(8,128)S(1)}, bf16[4,128,64]{1,2,0:T(8,128)(2,1)}, bf16[4,128,64]{1,2,0:T(8...) while((s32[]{:T(128)}, f32[4,128,8,64]{1,3,2,0:T(8,128)}, ...), condition=%wide.region_9.10_spmd.clone, body=%wide.region_7.9_spmd.sunk.clone | while | flops 85739776 | bytes 6718569 | solution.py:241
  349.0 0.7 dynamic-slice_bitcast_fusion.3
  349.7 1.2 fusion.187
  350.9 1.2 convolution_bitcast_fusion.7
  352.1 1.0 fusion.188
  353.1 1.2 fusion.189
  354.3 1.7 fusion.190
  356.0 0.7 dynamic-slice_bitcast_fusion.3
  356.7 1.2 fusion.187
  357.9 1.2 convolution_bitcast_fusion.7
  359.1 1.0 fusion.188
  360.1 1.2 fusion.189
  361.3 1.7 fusion.190
  363.0 0.7 dynamic-slice_bitcast_fusion.3
  363.7 1.2 fusion.187
  364.9 1.2 convolution_bitcast_fusion.7
  366.1 1.0 fusion.188
  367.1 1.2 fusion.189
  368.3 1.7 fusion.190
  370.0 0.7 dynamic-slice_bitcast_fusion.3
  370.7 1.2 fusion.187
  371.9 1.2 convolution_bitcast_fusion.7
  373.1 1.0 fusion.188
  374.1 1.2 fusion.189
  375.3 1.7 fusion.190
  377.0 1.5 bitcast_multiply_fusion
  379.0 0.7 copy-done.13
  379.7 6.6 convolution_convert_fusion.2
  386.3 1.3 copy-done.1
  387.6 12.1 %convolution_convert_fusion.1 = bf16[5632,2048]{1,0:T(8,128)(2,1)} fusion(bf16[128,5632]{1,0:T(8,128)(2,1)S(1)} %copy-done.1, bf16[128,2048]{1,0:T(8,128)(2,1)} %param.23, f32[128]{0:T(128)} %compare_convert_fusion), kind=kOutput, calls=%fused_computation.73 | convolution fusion | flops 2965110784 | bytes 25035264 | tf_op jit(solution)/shard_map/dot_general | solution.py:58
  399.8 31.5 %convolution_convert_fusion = bf16[2048,11264]{1,0:T(8,128)(2,1)} fusion(bf16[128,5632]{1,0:T(8,128)(2,1)} %get-tuple-element.160, bf16[128,5632]{1,0:T(8,128)(2,1)} %get-tuple-element.159, f32[128,2048]{1,0:T(8,128)S(1)} %get-tuple-element.179, f32[2048]{0:T(1024)S(1)} %bitcast.194, f32[128]{0:T(128)} %copy-done.25), kind=kOutput, calls=%fused_computation.68 | convolution fusion | flops 5935202304 | bytes 50078208 | tf_op jit(solution)/shard_map/dot_general | solution.py:58
  431.4 9.4 fusion.89
  441.5 66.4 %psum.39 = f32[2,2048]{1,0:T(2,128)} all-reduce(f32[2,2048]{1,0:T(2,128)} %pad_maximum_fusion.9), channel_id=1, replica_groups=mesh['fsdp_0'=4,'fsdp_1'=4,'fsdp_2'=2,'rep'=4] {'fsdp_0','fsdp_1','fsdp_..., use_global_device_ids=true, to_apply=%region_21.22 | all-reduce | flops 4096 | bytes 32768 | tf_op jit(solution)/shard_map/psum | solution.py:263
  507.9 1.4 multiply_subtract_fusion.4
  509.3 27.0 %reduce-scatter.5.cloned.1.call-done = bf16[64,2560]{1,0:T(8,128)(2,1)} async-done(((bf16[2048,2560]{1,0:T(8,128)(2,1)}), bf16[64,2560]{1,0:T(8,128)(2,1)}) %reduce-scatter.5.cloned.1.call-update) | async-done | bytes 327696 | tf_op jit(solution)/shard_map/reduce_scatter | solution.py:36
  536.3 137.0 %reduce-scatter.11.cloned.1.call-done = bf16[176,2048]{1,0:T(8,128)(2,1)} async-done(((bf16[5632,2048]{1,0:T(8,128)(2,1)}), bf16[176,2048]{1,0:T(8,128)(2,1)}) %reduce-scatter.11.cloned.1.call-update) | async-done | bytes 720912 | tf_op jit(solution)/shard_map/reduce_scatter | solution.py:36
  673.3 208.8 %reduce-scatter.9.cloned.1.call-done = bf16[64,11264]{1,0:T(8,128)(2,1)} async-done(((bf16[2048,11264]{1,0:T(8,128)(2,1)}), bf16[64,11264]{1,0:T(8,128)(2,1)}) %reduce-scatter.9.cloned.1.call-update) | async-done | bytes 1441808 | tf_op jit(solution)/shard_map/reduce_scatter | solution.py:36
  882.8 2.8 fusion.86
  885.6 11.6 %fusion.78 = bf16[128,2048]{1,0:T(8,128)(2,1)} fusion(f32[128,2048]{1,0:T(8,128)S(1)} %get-tuple-element.179, bf16[128,5632]{1,0:T(8,128)(2,1)S(1)} %copy-done.1, bf16[5632,2048]{1,0:T(8,128)(2,1)} %all-gather.5.cloned.1.call-done, f32[128]{0:T(128)S(1)} %copy-done.28), kind=kOutput, calls=%fused_computation.99 | convolution fusion | flops 2953576448 | bytes 26083840 | tf_op jit(solution)/shard_map/dot_general | solution.py:46
  897.3 57.4 %all-reduce.3.cloned.1.call-done = (bf16[64,2560]{1,0:T(8,128)(2,1)}, bf16[64,2048]{1,0:T(8,128)(2,1)}, bf16[64,11264]{1,0:T(8,128)(2,1)}, bf16[176,2048]{1,0:T(8,128)(2,1)}) async-done(((bf16[64,2560]{1,0:T(8,128)(2,1)}, bf16[64,2048]{1,0:T(8,128)(2,1)}, bf16[64,11264]{1,0:T(8,128)(2,1)}, bf16[176,2048]{1,0:T(8,128)(2,1)}), (bf16[64,2560]{1,0:T(8,128)(2,1)}, bf16[64,2048]{1,0:T(8,128)(2,1)}, ...) | async-done | bytes 2752528 | tf_op jit(solution)/shard_map/psum | solution.py:265
  954.7 3.1 multiply_subtract_fusion.2
  957.8 1.4 multiply_subtract_fusion.3
  959.3 7.4 multiply_subtract_fusion
  966.7 2.8 multiply_subtract_fusion.1
  (128 shorter events, 8.9 us)
Async XLA Ops:
  7.2 2.1 copy-start.14
  7.2 2.2 copy-start.10
  7.2 199.2 %all-gather.3.cloned.1.call-start = ((), (), s32[]{:S(2)}) async-start(), calls=%async_computation.4 | async-start | bytes 67043328 | tf_op jit(solution)/shard_map/all_gather | solution.py:28
  9.4 2.1 copy-start.4
  10.8 3.1 copy-start.2
  10.8 3.8 copy-start.24
  10.9 285.7 %all-gather.5.cloned.1.call-start = ((), (), s32[]{:S(2)}) async-start(), calls=%async_computation.5 | async-start | bytes 23789568 | tf_op jit(solution)/shard_map/all_gather | solution.py:182
  12.4 496.9 %reduce-scatter.7.cloned.1.call-start = ((), (), s32[]{:S(2)}) async-start(), calls=%async_computation.7 | async-start | bytes 8650752 | tf_op jit(solution)/shard_map/reduce_scatter | solution.py:36
  14.7 196.8 %copy-start.29 = (f32[128]{0:T(128)}, f32[128]{0:T(128)S(1)}, u32[]{:S(2)}) copy-start(f32[128]{0:T(128)S(1)} %get-tuple-element.175) | copy-start | bytes 1540
  221.9 4.9 copy-start.7
  226.9 107.5 %copy-start.25 = (f32[128]{0:T(128)}, f32[128]{0:T(128)S(1)}, u32[]{:S(2)}) copy-start(f32[128]{0:T(128)S(1)} %get-tuple-element.177) | copy-start | bytes 1540
  226.9 69.7 %copy-start.12 = (bf16[128,2048]{1,0:T(8,128)(2,1)S(1)}, bf16[128,2048]{1,0:T(8,128)(2,1)}, u32[]{:S(2)}) copy-start(bf16[128,2048]{1,0:T(8,128)(2,1)} %param.23) | copy-start | bytes 1572868
  226.9 69.7 %copy-start.27 = (f32[128]{0:T(128)S(1)}, f32[128]{0:T(128)}, u32[]{:S(2)}) copy-start(f32[128]{0:T(128)} %compare_convert_fusion) | copy-start | bytes 1540
  334.4 1.7 copy-start.8
  341.7 194.7 %reduce-scatter.5.cloned.1.call-start = ((), (), s32[]{:S(2)}) async-start(), calls=%async_computation.6 | async-start | bytes 10813440 | tf_op jit(solution)/shard_map/reduce_scatter | solution.py:36
  377.0 1.7 copy-start.6
  378.6 1.1 copy-start.3
  378.6 1.1 copy-start.23
  378.6 1.1 copy-start.30
  378.9 0.8 copy-start.13
  378.9 7.3 copy-start.21
  386.3 1.4 copy-start.1
  386.3 287.1 %reduce-scatter.11.cloned.1.call-start = ((), (), s32[]{:S(2)}) async-start(), calls=%async_computation.9 | async-start | bytes 23789568 | tf_op jit(solution)/shard_map/reduce_scatter | solution.py:36
  399.7 482.4 %reduce-scatter.9.cloned.1.call-start = ((), (), s32[]{:S(2)}) async-start(), calls=%async_computation.8 | async-start | bytes 47579136 | tf_op jit(solution)/shard_map/reduce_scatter | solution.py:36
  431.3 9.5 copy-start.26
  431.4 523.3 %all-reduce.3.cloned.1.call-start = ((), (), s32[]{:S(2)}) async-start(), calls=%async_computation.10 | async-start | bytes 5505024 | tf_op jit(solution)/shard_map/psum | solution.py:265
  882.1 3.5 copy-start.28
  885.6 69.1 %copy-start.11 = (f32[64,2560]{1,0:T(8,128)S(1)}, f32[64,2560]{1,0:T(8,128)}, u32[]{:S(2)}) copy-start(f32[64,2560]{1,0:T(8,128)} %param.25) | copy-start | bytes 1966084
  897.2 60.6 %copy-start.15 = (f32[64,2048]{1,0:T(8,128)S(1)}, f32[64,2048]{1,0:T(8,128)}, u32[]{:S(2)}) copy-start(f32[64,2048]{1,0:T(8,128)} %param.28) | copy-start | bytes 1572868
  897.3 60.6 %copy-start.19 = (f32[64,2048]{1,0:T(8,128)S(1)}, f32[64,2048]{1,0:T(8,128)}, u32[]{:S(2)}) copy-start(f32[64,2048]{1,0:T(8,128)} %param.30) | copy-start | bytes 1572868
  897.3 60.6 %copy-start.20 = (f32[64,2048]{1,0:T(8,128)S(1)}, f32[64,2048]{1,0:T(8,128)}, u32[]{:S(2)}) copy-start(f32[64,2048]{1,0:T(8,128)} %param.29) | copy-start | bytes 1572868
  954.7 3.1 copy-start.22
  954.7 4.5 copy-start
  954.7 4.5 copy-start.9
  959.2 7.4 copy-start.5
  959.2 7.4 copy-start.16
  959.2 7.4 copy-start.17
  959.2 7.4 copy-start.18
Sparse Core Ops, SparseCore 0:
  11.0 195.4 all-gather.2
  209.3 87.2 all-gather.4
  341.8 92.3 reduce-scatter.6
  438.3 97.9 reduce-scatter.4
  540.2 133.1 reduce-scatter.10
  677.7 204.4 reduce-scatter.8
  884.9 69.7 all-reduce.2
where the time goes:
time: 988 us; the launch traced here: 976 us
  waiting for transfers between devices  672 us (68%)
  matrix products  181 us (18%)
  blocking collectives  66.4 us (7%)
  other arithmetic  33.7 us (3%)
  between operations  15.4 us (2%)
    reduce_scatter x4, waiting for transfers between devices, reduce_rows(): lax.psum_scatter(term_fn(jnp.int32(0), shard_rows * lax.axis_size(FSDP))....  373 us
    all_gather x1, waiting for transfers between devices, in_one_piece(): out, at, done = (lax.all_gather(both, axis, axis=dim, tiled=True), 0, [])  192 us
    psum x1, blocking collectives, body(): lax.psum(jnp.stack([first_gain_grad, second_gain_grad]), FSDP_REP)  66.4 us
    psum x1, waiting for transfers between devices, body(): lax.psum(qkv_grad.astype(jnp.bfloat16), 'rep').astype(jnp.float32)  57.4 us
    dot_general x4, matrix products, term_fn(): lax.dot_general(source, grads, (((0,), (0,)), ((), ())), preferred_elemen...  55.8 us
    dot_general x4, matrix products, apply_backward(): lax.dot_general(source, whole, (((1,), (1,)), ((), ())), preferred_elemen...  53.5 us
    all_gather x1, waiting for transfers between devices, body(): lax.all_gather(down_low, FSDP, axis=0, tiled=True)  49.9 us
    dot_general x4, matrix products, apply_forward(): return jnp.dot(source, whole, preferred_element_type=jnp.float32)  41.2 us
  transfers between devices with their start and end apart: 7, of which 6 were waited for; matrix products, arithmetic and copies ran while one was open for 16% of the time, Pallas kernels for 0%

commit v1 on v0

v1 whole, which is shorter than its diff:
```python
import functools

import jax
import jax.numpy as jnp
from jax import lax
from jax.experimental import pallas as pl
from jax.experimental.pallas import tpu as pltpu
from jax.sharding import Mesh
from jax.sharding import PartitionSpec as P

QUERY_HEADS = 32
KEY_VALUE_HEADS = 4
HEAD_SIZE = 64
FF = 5632
STEP = 10
GROUP = 4
WIDTH = QUERY_HEADS * HEAD_SIZE
KV_WIDTH = KEY_VALUE_HEADS * HEAD_SIZE
HEADS = QUERY_HEADS // GROUP
Q_COLS = WIDTH // GROUP
KV_COLS = KV_WIDTH // GROUP
FF_COLS = FF // GROUP
FSDP = ("fsdp_0", "fsdp_1", "fsdp_2")
FSDP_REP = ("fsdp_0", "fsdp_1", "fsdp_2", "rep")

norm_epsilon = 1e-05
beta_one = 0.9
beta_two = 0.999
adam_epsilon = 1e-08
matrix_rate = 0.02
matrix_decay = 0.1
gain_rate = 0.5
masked_score = -1e30
f32 = jnp.float32
bf16 = jnp.bfloat16

TURN = [(z * GROUP + x, x * GROUP + z) for z in range(GROUP) for x in range(GROUP)]


def dot(a, b, ca, cb):
    return lax.dot_general(a, b, (((ca,), (cb,)), ((), ())), preferred_element_type=f32)


def fetch(block, k):
    return lax.ppermute(block, "rep", [((i + k) % GROUP, i) for i in range(GROUP)])


def send(block, k):
    return lax.ppermute(block, "rep", [(i, (i + k) % GROUP) for i in range(GROUP)])


def gather_rows(block):
    return jnp.concatenate([block] + [fetch(block, k) for k in range(1, GROUP)], axis=0)


def scatter_rows(partial, rows):
    total = partial[:rows]
    low = partial.astype(bf16)
    for k in (2, 1, 3):
        total = total + send(low[k * rows : (k + 1) * rows], k).astype(f32)
    return total


def turn(piece):
    return lax.ppermute(piece, ("fsdp_0", "rep"), TURN)


def spread(block):
    return lax.all_gather(block, FSDP, axis=0, tiled=True)


def sum_along(block, axis, dim, dtype):
    here = lax.axis_index(axis)

    def entry(k):
        return lax.dynamic_index_in_dim(block, (here + k) % GROUP, dim, keepdims=False)

    total = entry(0).astype(f32)
    for k in (2, 1, 3):
        perm = [(i, (i + k) % GROUP) for i in range(GROUP)]
        total = total + lax.ppermute(entry(k), axis, perm).astype(f32)
    return total.astype(dtype)


def collect(partial, first):
    low = partial.astype(bf16).reshape(GROUP, GROUP, 2, -1, partial.shape[-1])
    core = lax.axis_index("fsdp_2")
    other = lax.dynamic_index_in_dim(low, 1 - core, 2, keepdims=False)
    own = lax.dynamic_index_in_dim(low, core, 2, keepdims=False)
    other = lax.ppermute(other, "fsdp_2", [(0, 1), (1, 0)])
    pair = (own.astype(f32) + other.astype(f32)).astype(bf16)
    if first == "fsdp_0":
        return sum_along(sum_along(pair, "fsdp_0", 0, bf16), "fsdp_1", 0, bf16)
    return sum_along(sum_along(pair, "fsdp_1", 1, bf16), "fsdp_0", 0, bf16)


def collect_far(partial):
    return lax.psum_scatter(partial.astype(bf16), FSDP, scatter_dimension=0, tiled=True)


def share(piece):
    return [piece] + [fetch(piece, k) for k in range(1, GROUP)]


def share_turned(piece):
    out = []
    for k in range(GROUP):
        perm = [
            (z * GROUP + x, x * GROUP + (z - k) % GROUP) for z in range(GROUP) for x in range(GROUP)
        ]
        out.append(lax.ppermute(piece, ("fsdp_0", "rep"), perm))
    return out


def norm_inverse(values):
    return lax.rsqrt(jnp.mean(values * values, axis=-1, keepdims=True) + norm_epsilon)


def norm_backward(values, inverse, gain, grads):
    scaled = grads * gain
    return inverse * scaled - values * (inverse * inverse * inverse) * jnp.mean(
        scaled * values, axis=-1, keepdims=True
    )


def rotary_tables(token_count):
    positions = jnp.arange(token_count, dtype=f32)
    exponents = jnp.arange(0, HEAD_SIZE, 2, dtype=f32) / HEAD_SIZE
    freqs = jnp.power(10000.0, -exponents)
    angles = positions[:, None] * freqs[None, :]
    angles = jnp.concatenate([angles, angles], axis=-1)[:, None, :]
    return (jnp.cos(angles), jnp.sin(angles))


def rotate_pairs(values, cosine_table, sine_table):
    half = values.shape[-1] // 2
    turned = jnp.concatenate([-values[..., half:], values[..., :half]], axis=-1)
    return values * cosine_table + turned * sine_table


def unrotate(values, cosine_table, sine_table):
    half = values.shape[-1] // 2
    product = values * sine_table
    turned = jnp.concatenate([product[..., half:], -product[..., :half]], axis=-1)
    return values * cosine_table + turned


def causal_scores(query, key):
    count = query.shape[1]
    scores = jnp.einsum("bthd,bsd->bhts", query, key, preferred_element_type=f32)
    scores = scores * HEAD_SIZE ** (-0.5)
    row_index = lax.broadcasted_iota(jnp.int32, (count, count), 0)
    col_index = lax.broadcasted_iota(jnp.int32, (count, count), 1)
    return jnp.where(row_index >= col_index, scores, masked_score)


def attend(query, key, value):
    scores = causal_scores(query, key)
    top = jnp.max(scores, axis=-1, keepdims=True)
    expos = jnp.exp(scores - top)
    totals = jnp.sum(expos, axis=-1, keepdims=True)
    probs = (expos / totals).astype(bf16)
    mixed = jnp.einsum("bhts,bsd->bthd", probs, value, preferred_element_type=f32)
    return mixed.astype(bf16), top + jnp.log(totals)


def attend_backward(query, key, value, grads, logsum):
    scores = causal_scores(query, key)
    probs = jnp.exp(scores - logsum)
    value_grad = jnp.einsum("bhts,bthd->bsd", probs.astype(bf16), grads, preferred_element_type=f32)
    prob_grad = jnp.einsum("bthd,bsd->bhts", grads, value, preferred_element_type=f32)
    delta = jnp.sum(prob_grad * probs, axis=-1, keepdims=True)
    score_grad = (probs * (prob_grad - delta) * HEAD_SIZE ** (-0.5)).astype(bf16)
    query_grad = jnp.einsum("bhts,bsd->bthd", score_grad, key, preferred_element_type=f32)
    key_grad = jnp.einsum("bhts,bthd->bsd", score_grad, query, preferred_element_type=f32)
    return query_grad, key_grad, value_grad


def adamw(weight, grad, moment, second, rate, decay):
    moment = beta_one * moment + (1.0 - beta_one) * grad
    second = beta_two * second + (1.0 - beta_two) * grad * grad
    fix_one = 1.0 - beta_one**STEP
    fix_two = 1.0 - beta_two**STEP
    weight = weight - rate * (
        moment / fix_one / (jnp.sqrt(second / fix_two) + adam_epsilon) + decay * weight
    )
    return (moment, second, weight)


def chosen(order, pieces):
    low = jnp.where(order == 0, pieces[0], pieces[1])
    high = jnp.where(order == 2, pieces[2], pieces[3])
    return jnp.where(order < 2, low, high)


def adam_kernel(spans, place, p0, p1, p2, p3, weight, moment, second, m_out, s_out, w_out):
    pieces = (p0, p1, p2, p3)
    for column, at, width in spans:
        grads = []
        for j in range(GROUP):
            order = (j + GROUP - place[0]) % GROUP
            grads.append(chosen(order, [p[:, at : at + width].astype(f32) for p in pieces]))
        if width % 128:
            blocks = [(column, GROUP * width, jnp.concatenate(grads, axis=1))]
        else:
            blocks = [(column + j * width, width, grads[j]) for j in range(GROUP)]
        for start, size, grad in blocks:
            cols = slice(start, start + size)
            new = adamw(
                weight[:, cols], grad, moment[:, cols], second[:, cols], matrix_rate, matrix_decay
            )
            m_out[:, cols], s_out[:, cols], w_out[:, cols] = new


def adam_step(spans, place, pieces, weight, moment, second, tile):
    rows, columns = weight.shape
    wide = pl.BlockSpec((tile, columns), lambda i, place: (i, 0))
    narrow = pl.BlockSpec((tile, pieces[0].shape[1]), lambda i, place: (i, 0))
    shape = jax.ShapeDtypeStruct(weight.shape, f32)
    return pl.pallas_call(
        functools.partial(adam_kernel, spans),
        grid_spec=pltpu.PrefetchScalarGridSpec(
            num_scalar_prefetch=1,
            grid=(rows // tile,),
            in_specs=[narrow] * 4 + [wide] * 3,
            out_specs=[wide] * 3,
        ),
        out_shape=[shape] * 3,
        compiler_params=pltpu.CompilerParams(vmem_limit_bytes=48 * 1024 * 1024),
        cost_estimate=pl.CostEstimate(
            flops=12 * rows * columns, bytes_accessed=26 * rows * columns, transcendentals=0
        ),
    )(place.reshape(1), *pieces, weight, moment, second)


def body(
    tokens,
    cotangent,
    lengths,
    qkv_weight,
    qkv_moment,
    qkv_second,
    out_weight,
    out_moment,
    out_second,
    gateup_weight,
    gateup_moment,
    gateup_second,
    down_weight,
    down_moment,
    down_second,
    gains,
    gain_moment,
    gain_second,
):
    count = tokens.shape[0]
    rows = count * GROUP
    place = lax.axis_index("rep")
    inputs = tokens.astype(f32)
    positions = jnp.arange(count, dtype=jnp.int32)
    valid = (positions < lengths[0]).astype(f32)[:, None]
    result_grad = cotangent.astype(f32) * valid
    output_low = result_grad.astype(bf16)
    cosine_table, sine_table = rotary_tables(count)

    def cut(weight, start, width):
        return lax.dynamic_slice_in_dim(weight, start + place * width, width, axis=1).astype(bf16)

    qkv_part = jnp.concatenate(
        [
            cut(qkv_weight, 0, Q_COLS),
            cut(qkv_weight, WIDTH, KV_COLS),
            cut(qkv_weight, WIDTH + KV_WIDTH, KV_COLS),
        ],
        axis=1,
    )
    quarter = out_weight.shape[1] // GROUP
    out_rows = out_weight.shape[0]
    turned = turn(
        jnp.concatenate([cut(out_weight, 0, quarter), cut(down_weight, 0, quarter)], axis=0)
    )
    near = spread(jnp.concatenate([qkv_part, turned[:out_rows]], axis=1))
    qkv = near[:, : qkv_part.shape[1]]
    out = near[:, qkv_part.shape[1] :].reshape(GROUP, -1, quarter)
    gateup = spread(
        jnp.concatenate([cut(gateup_weight, 0, FF_COLS), cut(gateup_weight, FF, FF_COLS)], axis=1)
    )
    down = spread(turned[out_rows:]).reshape(GROUP, -1, quarter)

    both = gather_rows(jnp.concatenate([tokens, output_low], axis=1))
    group_inputs = both[:, :WIDTH].astype(f32)
    group_low = both[:, WIDTH:]

    group_inverse = norm_inverse(group_inputs)
    first_low = (group_inputs * group_inverse * gains[0]).astype(bf16)
    joined = dot(first_low, qkv, 1, 0)
    query = rotate_pairs(
        joined[:, :Q_COLS].reshape(GROUP, count, HEADS, HEAD_SIZE), cosine_table, sine_table
    ).astype(bf16)
    key = rotate_pairs(
        joined[:, Q_COLS : Q_COLS + KV_COLS].reshape(GROUP, count, 1, HEAD_SIZE),
        cosine_table,
        sine_table,
    ).astype(bf16)[:, :, 0]
    value = joined[:, Q_COLS + KV_COLS :].reshape(GROUP, count, HEAD_SIZE).astype(bf16)
    mixed, logsum = attend(query, key, value)
    mixed_low = mixed.reshape(rows, Q_COLS)
    branch = dot(mixed_low, out, 1, 1).reshape(rows, WIDTH)
    middle = inputs + scatter_rows(branch, count)
    second_inverse = norm_inverse(middle)
    second_low = gather_rows((middle * second_inverse * gains[1]).astype(bf16))
    wide = dot(second_low, gateup, 1, 0)
    gate = wide[:, :FF_COLS]
    up_part = wide[:, FF_COLS:]
    hidden_low = (jax.nn.silu(gate) * up_part).astype(bf16)
    output = dot(hidden_low, down, 1, 1).reshape(rows, WIDTH)
    block_output = ((middle + scatter_rows(output, count)) * valid).astype(bf16)

    hidden_grad = sum(
        dot(group_low[:, j * quarter : (j + 1) * quarter], down[j], 1, 1) for j in range(GROUP)
    )
    sigma = jax.nn.sigmoid(gate)
    gate_grad = hidden_grad * up_part * sigma * (1.0 + gate * (1.0 - sigma))
    up_grad = hidden_grad * jax.nn.silu(gate)
    wide_grad = jnp.concatenate([gate_grad, up_grad], axis=1).astype(bf16)
    second_grad = scatter_rows(dot(wide_grad, gateup, 1, 1), count)
    down_piece = collect_far(
        lax.dot_general(
            group_low.reshape(rows, GROUP, quarter),
            hidden_low,
            (((0,), (0,)), ((), ())),
            preferred_element_type=f32,
        ).transpose(0, 2, 1).reshape(GROUP * FF_COLS, quarter)
    )
    gateup_piece = collect_far(dot(second_low, wide_grad, 0, 0))
    second_gain_grad = jnp.sum(second_grad * middle * second_inverse, axis=0)
    middle_grad = result_grad + norm_backward(middle, second_inverse, gains[1], second_grad)
    branch_low = gather_rows(middle_grad.astype(bf16))

    mixed_grad = sum(
        dot(branch_low[:, j * quarter : (j + 1) * quarter], out[j], 1, 1) for j in range(GROUP)
    ).astype(bf16)
    out_terms = (
        lax.dot_general(
            branch_low.reshape(rows, GROUP, quarter),
            mixed_low,
            (((0,), (0,)), ((), ())),
            preferred_element_type=f32,
        ).transpose(0, 2, 1).reshape(GROUP * Q_COLS, quarter)
    )
    query_grad, key_grad, value_grad = attend_backward(
        query, key, value, mixed_grad.reshape(GROUP, count, HEADS, HEAD_SIZE), logsum
    )
    joined_grad = jnp.concatenate(
        [
            unrotate(query_grad, cosine_table, sine_table).reshape(rows, Q_COLS),
            unrotate(key_grad[:, :, None], cosine_table, sine_table).reshape(rows, KV_COLS),
            value_grad.reshape(rows, KV_COLS),
        ],
        axis=1,
    ).astype(bf16)
    qkv_terms = dot(first_low, joined_grad, 0, 0)
    first_partial = dot(joined_grad, qkv, 1, 1)
    first_gain_grad = jnp.sum(first_partial * group_inputs * group_inverse, axis=0)
    first_grad = scatter_rows(first_partial, count)
    input_grad = middle_grad + norm_backward(inputs, group_inverse[:count], gains[0], first_grad)
    gain_rows = qkv_weight.shape[0]
    gain_terms = jnp.stack([first_gain_grad, second_gain_grad]).reshape(gain_rows, -1)
    gain_terms = jnp.tile(gain_terms, (qkv_terms.shape[0] // gain_rows, 1))
    near_piece = collect(jnp.concatenate([qkv_terms, out_terms, gain_terms], axis=1), "fsdp_0")
    qkv_cols = qkv_terms.shape[1]
    out_piece = near_piece[:, qkv_cols : qkv_cols + quarter]
    qkv_pieces = share(
        jnp.concatenate([near_piece[:, :qkv_cols], near_piece[:, qkv_cols + quarter :]], axis=1)
    )
    gain_grad = sum(p[:, qkv_cols:].astype(f32) for p in qkv_pieces).reshape(gains.shape)

    qkv_spans = (
        (0, 0, Q_COLS),
        (WIDTH, Q_COLS, KV_COLS),
        (WIDTH + KV_WIDTH, Q_COLS + KV_COLS, KV_COLS),
    )
    down_new = adam_step(
        ((0, 0, quarter),), place, share_turned(down_piece), down_weight, down_moment, down_second, 88
    )
    gateup_new = adam_step(
        ((0, 0, FF_COLS), (FF, FF_COLS, FF_COLS)),
        place,
        share(gateup_piece),
        gateup_weight,
        gateup_moment,
        gateup_second,
        16,
    )
    out_new = adam_step(
        ((0, 0, quarter),), place, share_turned(out_piece), out_weight, out_moment, out_second, 32
    )
    qkv_new = adam_step(
        qkv_spans, place, qkv_pieces, qkv_weight, qkv_moment, qkv_second, 32
    )
    gain_new = adamw(gains, gain_grad, gain_moment, gain_second, gain_rate, 0.0)
    return (
        block_output,
        input_grad,
        *qkv_new,
        *out_new,
        *gateup_new,
        *down_new,
        *gain_new,
    )


def solution(mesh):
    finer = Mesh(
        mesh.devices.reshape(4, 4, 2, mesh.shape["rep"]), ("fsdp_0", "fsdp_1", "fsdp_2", "rep")
    )
    row = P(FSDP_REP, None)
    weight = P(FSDP, None)
    return jax.shard_map(
        body,
        mesh=finer,
        in_specs=(row, row, P(FSDP_REP)) + (weight,) * 12 + (P(),) * 3,
        out_specs=(row, row) + (weight,) * 12 + (P(),) * 3,
        check_vma=False,
    )
```

time: 988 us -> 516 us (0.52)
  waiting for transfers between devices: 672 us -> 188 us
  starting transfers between devices: 0.29 us -> 76.5 us
  matrix products: 181 us -> 105 us
  blocking collectives: 66.4 us -> 0 us
  local copies, waits for them, and re-layouts: 7.07 us -> 70 us
  Pallas kernels: 0 us -> 15.2 us
    reduce_scatter x4 -> x2, waiting for transfers between devices: 373 us -> 0.01 us  [collect_far(): lax.psum_scatter(partial.astype(bf16), FSDP, scatter_dimension=0, tiled=T...]
    all_gather x2 -> x3, waiting for transfers between devices: 242 us -> 20 us  [spread(): return lax.all_gather(block, FSDP, axis=0, tiled=True)]
    ppermute x0 -> x43, waiting for transfers between devices: none -> 168 us  [the longest x15 84.3 us: fetch(): lax.ppermute(block, 'rep', [((i + k) % GROUP, i) for i in range(GROUP)])]
    dot_general x40 -> x24, matrix products: 181 us -> 105 us  [the longest x16 87.7 us: dot(): lax.dot_general(a, b, (((ca,), (cb,)), ((), ())), preferred_element_type=...]
    ppermute x0 -> x43, starting transfers between devices: none -> 66.7 us  [the longest x8 21.8 us: share_turned(): out.append(lax.ppermute(piece, ('fsdp_0', 'rep'), perm))]
    psum x1 -> x0, blocking collectives: 66.4 us -> none  [body(): lax.psum(jnp.stack([first_gain_grad, second_gain_grad]), FSDP_REP)]
    psum x1 -> x0, waiting for transfers between devices: 57.4 us -> none  [body(): lax.psum(qkv_grad.astype(jnp.bfloat16), 'rep').astype(jnp.float32)]
    slice x7 -> x29, local copies, waits for them, and re-layouts: 0.64 us -> 33 us  [the longest x10 17.6 us: scatter_rows(): total = total + send(low[k * rows:(k + 1) * rows], k).astype(f32)]
  transfers between devices with their start and end apart: 7 -> 48, of which waited for: 6 -> 24; matrix products, arithmetic and copies ran while one was open for 16% -> 34% of each run, Pallas kernels for 0% -> 2%
where the time goes in v1:
time: 516 us; the launch traced here: 510 us
  waiting for transfers between devices  188 us (36%)
  matrix products  105 us (20%)
  starting transfers between devices  76.5 us (15%)
  local copies, waits for them, and re-layouts  70 us (14%)
  other arithmetic  39.3 us (8%)
  between operations  15.6 us (3%)
  Pallas kernels  15.2 us (3%)
    dot_general x16, matrix products, dot(): lax.dot_general(a, b, (((ca,), (cb,)), ((), ())), preferred_element_type=...  87.7 us
    ppermute x15, waiting for transfers between devices, fetch(): lax.ppermute(block, 'rep', [((i + k) % GROUP, i) for i in range(GROUP)])  84.3 us
    ppermute x12, waiting for transfers between devices, send(): lax.ppermute(block, 'rep', [(i, (i + k) % GROUP) for i in range(GROUP)])  37.6 us
    ppermute x6, waiting for transfers between devices, sum_along(): total = total + lax.ppermute(entry(k), axis, perm).astype(f32)  23.6 us
    ppermute x8, starting transfers between devices, share_turned(): out.append(lax.ppermute(piece, ('fsdp_0', 'rep'), perm))  21.8 us
    all_gather x3, waiting for transfers between devices, spread(): return lax.all_gather(block, FSDP, axis=0, tiled=True)  20 us
    ppermute x12, starting transfers between devices, send(): lax.ppermute(block, 'rep', [(i, (i + k) % GROUP) for i in range(GROUP)])  18.1 us
    slice x10, local copies, waits for them, and re-layouts, scatter_rows(): total = total + send(low[k * rows:(k + 1) * rows], k).astype(f32)  17.6 us
  transfers between devices with their start and end apart: 48, of which 24 were waited for; matrix products, arithmetic and copies ran while one was open for 34% of the time, Pallas kernels for 2%

profile of v1, /device:TPU:96, one launch (start us, length us, event | category | flops | bytes accessed | tf_op | source)
XLA Modules:
  0.0 509.6 jit_solution(14701381335563084300)
XLA Ops:
  9.3 3.3 collective-permute-start.3
  14.4 13.1 %collective-permute-done.3 = bf16[240,512]{1,0:T(8,128)(2,1)S(1)} collective-permute-done((bf16[240,512]{1,0:T(8,128)(2,1)S(1)}, bf16[240,512]{1,0:T(8,128)(2,1)S(1)}, u32[]{:S(2)}, u32[]{:S(2)}) %collective-permute-start.3) | collective-permute-done | bytes 245792 | tf_op jit(solution)/shard_map/ppermute | solution.py:65
  34.3 23.8 %collective-permute-done = bf16[128,4096]{1,0:T(8,128)(2,1)S(1)} collective-permute-done((bf16[128,4096]{1,0:T(8,128)(2,1)S(1)}, bf16[128,4096]{1,0:T(8,128)(2,1)S(1)}, u32[]{:S(2)}, u32[]{:S(2)}) %collective-permute-start) | collective-permute-done | bytes 1048608 | tf_op jit(solution)/shard_map/ppermute | solution.py:45
  59.7 21.3 %collective-permute-done.2 = bf16[128,4096]{1,0:T(8,128)(2,1)S(1)} collective-permute-done((bf16[128,4096]{1,0:T(8,128)(2,1)S(1)}, bf16[128,4096]{1,0:T(8,128)(2,1)S(1)}, u32[]{:S(2)}, u32[]{:S(2)}) %collective-permute-start.2) | collective-permute-done | bytes 1048608 | tf_op jit(solution)/shard_map/ppermute | solution.py:45
  81.1 5.2 %pad_maximum_fusion.1 = bf16[512,4096]{1,0:T(8,128)(2,1)} fusion(bf16[128,4096]{1,0:T(8,128)(2,1)S(1)} %collective-permute-done.2, bf16[128,4096]{1,0:T(8,128)(2,1)S(1)} %collective-permute-done.1, bf16[128,4096]{1,0:T(8,128)(2,1)S(1)} %collective-permute-done, bf16[128,2048]{1,0:T(8,128)(2,1)S(1)} %fusion.68, bf16[128,2048]{1,0:T(8,128)(2,1)S(1)} %copy-done.11), kind=kLoop, calls=%fused_computation.14 | loop fusion | flops 20971520 | bytes 8388608 | tf_op jit(solution)/shard_map/concatenate | solution.py:53
  88.4 4.2 fusion.12
  100.9 3.3 fusion.156
  115.5 3.2 slice.344
  118.7 3.9 copy.114
  122.6 2.3 slice.306
  124.9 2.5 copy.74
  127.4 7.0 %collective-permute-done.5 = bf16[128,2048]{1,0:T(8,128)(2,1)} collective-permute-done((bf16[128,2048]{1,0:T(8,128)(2,1)}, bf16[128,2048]{1,0:T(8,128)(2,1)}, u32[]{:S(2)}, u32[]{:S(2)}) %collective-permute-start.5) | collective-permute-done | bytes 524320 | tf_op jit(solution)/shard_map/ppermute | solution.py:49
  134.5 3.1 multiply_reduce_fusion.2
  141.8 4.3 fusion.30
  146.1 4.0 fusion.32
  150.1 4.0 fusion.34
  154.8 2.2 collective-permute-done.8
  157.0 9.6 %collective-permute-done.9 = bf16[128,2048]{1,0:T(8,128)(2,1)} collective-permute-done((bf16[128,2048]{1,0:T(8,128)(2,1)}, bf16[128,2048]{1,0:T(8,128)(2,1)}, u32[]{:S(2)}, u32[]{:S(2)}) %collective-permute-start.9) | collective-permute-done | bytes 524320 | tf_op jit(solution)/shard_map/ppermute | solution.py:45
  166.6 19.9 %all-gather.6.cloned.1.call-done = bf16[2048,2816]{1,0:T(8,128)(2,1)} async-done(((bf16[64,2816]{1,0:T(8,128)(2,1)}), bf16[2048,2816]{1,0:T(8,128)(2,1)}) %all-gather.6.cloned.1.call-update) | async-done | bytes 11534352 | tf_op jit(solution)/shard_map/all_gather | solution.py:69
  186.6 10.2 %fusion.118 = f32[512,2816]{1,0:T(8,128)S(1)} fusion(bf16[2048,2816]{1,0:T(8,128)(2,1)} %all-gather.6.cloned.1.call-done, bf16[128,2048]{1,0:T(8,128)(2,1)} %collective-permute-done.9, bf16[128,2048]{1,0:T(8,128)(2,1)} %collective-permute-done.8, bf16[128,2048]{1,0:T(8,128)(2,1)} %collective-permute-done.7, bf16[128,2048]{1,0:T(8,128)(2,1)} %multiply_convert_fusion.4), kind=kOutput, calls=%fused_computation.168 | convolution fusion | flops 5913968640 | bytes 19398656 | tf_op jit(solution)/shard_map/dot_general | solution.py:41
  196.9 8.2 %multiply_convert_fusion.1 = (bf16[512,1408]{1,0:T(8,128)(2,1)}, bf16[512,1408]{1,0:T(8,128)(2,1)}, bf16[512,1408,1]{1,0,2:T(8,128)(2,1)S(1)}) fusion(f32[512,2816]{1,0:T(8,128)S(1)} %fusion.118, f32[512,1408]{1,0:T(8,128)S(1)} %copy-done.28, f32[512,1408]{1,0:T(8,128)S(1)} %copy-done.29, f32[512,1408]{1,0:T(8,128)S(1)} %copy-done.30, ...), kind=kOutput, calls=%fused_computation.21 | convolution fusion | flops 753795072 | bytes 24379392 | tf_op jit(solution)/shard_map/dot_general | solution.py:41
  206.2 5.2 %convert_bitcast_fusion = bf16[4,1408,512]{1,2,0:T(8,128)(2,1)} fusion(bf16[512,4,512]{0,2,1:T(8,128)(2,1)S(1)} %bitcast.189, bf16[512,1408,1]{1,0,2:T(8,128)(2,1)S(1)} %get-tuple-element.53), kind=kOutput, calls=%fused_computation.5 | convolution fusion | flops 2955673600 | bytes 9306112 | tf_op jit(solution)/shard_map/dot_general | solution.py:328
  211.4 8.2 %copy.96 = bf16[4,1408,512]{2,1,0:T(8,128)(2,1)} copy(bf16[4,1408,512]{1,2,0:T(8,128)(2,1)} %convert_bitcast_fusion) | data formatting | bytes 11534336 | tf_op jit(solution)/shard_map/convert_element_type | solution.py:98
  219.6 9.7 %reduce-scatter.3.cloned.1.call-start = ((), (), s32[]{:S(2)}) async-start(), calls=%async_computation.5 | async-start | bytes 11894784 | tf_op jit(solution)/shard_map/reduce_scatter | solution.py:98
  229.3 11.2 %convolution_convert_fusion = bf16[2048,2816]{1,0:T(8,128)(2,1)} fusion(bf16[512,1408]{1,0:T(8,128)(2,1)} %get-tuple-element.52, bf16[512,1408]{1,0:T(8,128)(2,1)} %get-tuple-element.51, bf16[128,2048]{1,0:T(8,128)(2,1)} %collective-permute-done.9, bf16[128,2048]{1,0:T(8,128)(2,1)} %collective-permute-done.8, bf16[128,2048]{1,0:T(8,128)(2,1)} %collective-permute-done.7, ...), kind=kOutput, calls=%fused_computation.1 | convolution fusion | flops 5925502976 | bytes 16515072 | tf_op jit(solution)/shard_map/dot_general | solution.py:41
  240.5 11.6 %fusion.157 = (bf16[512,2048]{1,0:T(8,128)(2,1)S(1)}, f32[512,2048]{1,0:T(8,128)}) fusion(bf16[2048,2816]{1,0:T(8,128)(2,1)} %all-gather.6.cloned.1.call-done, bf16[512,1408]{1,0:T(8,128)(2,1)} %get-tuple-element.52, bf16[512,1408]{1,0:T(8,128)(2,1)} %get-tuple-element.51), kind=kOutput, calls=%fused_computation.239 | convolution fusion | flops 5912395776 | bytes 20709376 | tf_op jit(solution)/shard_map/dot_general | solution.py:41
  253.3 3.0 collective-permute-start.13
  256.8 2.7 collective-permute-start.15
  259.5 8.9 %fusion.158 = (bf16[512,4,512]{0,2,1:T(8,128)(2,1)S(1)}, f32[512,4,512]{0,2,1:T(8,128)}) fusion(bf16[512,1408,1]{1,0,2:T(8,128)(2,1)S(1)} %copy-done.45, bf16[4,1408,512]{2,1,0:T(8,128)(2,1)} %bitcast.186), kind=kOutput, calls=%fused_computation.240 | convolution fusion | flops 2953838592 | bytes 13500416 | tf_op jit(solution)/shard_map/dot_general | solution.py:41
  275.8 2.4 slice.313
  278.1 2.6 copy.79
  280.7 2.4 collective-permute-start.12
  283.1 2.6 multiply_reduce_fusion
  285.7 6.7 %collective-permute-done.10 = bf16[128,2048]{1,0:T(8,128)(2,1)} collective-permute-done((bf16[128,2048]{1,0:T(8,128)(2,1)}, bf16[128,2048]{1,0:T(8,128)(2,1)}, u32[]{:S(2)}, u32[]{:S(2)}) %collective-permute-start.10) | collective-permute-done | bytes 524320 | tf_op jit(solution)/shard_map/ppermute | solution.py:49
  292.4 10.5 %collective-permute-done.11 = bf16[128,2048]{1,0:T(8,128)(2,1)} collective-permute-done((bf16[128,2048]{1,0:T(8,128)(2,1)}, bf16[128,2048]{1,0:T(8,128)(2,1)}, u32[]{:S(2)}, u32[]{:S(2)}) %collective-permute-start.11) | collective-permute-done | bytes 524320 | tf_op jit(solution)/shard_map/ppermute | solution.py:49
  302.9 3.7 fusion.146
  306.6 2.6 collective-permute-start.16
  311.7 20.5 %collective-permute-done.16 = bf16[128,2048]{1,0:T(8,128)(2,1)} collective-permute-done((bf16[128,2048]{1,0:T(8,128)(2,1)}, bf16[128,2048]{1,0:T(8,128)(2,1)}, u32[]{:S(2)}, u32[]{:S(2)}) %collective-permute-start.16) | collective-permute-done | bytes 524320 | tf_op jit(solution)/shard_map/ppermute | solution.py:45
  332.1 3.7 collective-permute-done.18
  349.4 4.5 broadcast_multiply_fusion
  356.9 3.3 fusion.45
  361.5 7.5 %fusion.6 = (f32[2048]{0:T(1024)S(1)}, bf16[512,2048]{1,0:T(8,128)(2,1)}, f32[512,2048]{1,0:T(8,128)}) fusion(f32[512]{0:T(512)S(1)} %add_rsqrt_fusion, bf16[512,4096]{1,0:T(8,128)(2,1)} %pad_maximum_fusion.1, bf16[512,640]{0,1:T(8,128)(2,1)S(1)} %bitcast_dynamic-update-slice_fusion.1, bf16[2048,1152]{1,0:T(8,128)(2,1)} %all-gather.4.cloned.1.call-done), kind=kOutput, calls=%fused_computation.13 | convolution fusion | flops 1347418112 | bytes 11675648 | tf_op jit(solution)/shard_map/dot_general | solution.py:41
  370.4 3.6 convolution_convert_fusion.1
  374.8 2.3 copy-done.12
  377.6 2.6 fusion.148
  382.0 2.9 collective-permute-start.21
  384.9 3.4 fusion.1
  393.1 3.5 collective-permute-done.19
  397.3 9.9 %collective-permute-done.20 = bf16[128,2048]{1,0:T(8,128)(2,1)} collective-permute-done((bf16[128,2048]{1,0:T(8,128)(2,1)}, bf16[128,2048]{1,0:T(8,128)(2,1)}, u32[]{:S(2)}, u32[]{:S(2)}) %collective-permute-start.20) | collective-permute-done | bytes 524320 | tf_op jit(solution)/shard_map/ppermute | solution.py:49
  409.4 3.6 collective-permute-done.23
  413.0 12.2 %collective-permute-done.24 = bf16[4,64,1216]{2,1,0:T(8,128)(2,1)} collective-permute-done((bf16[4,64,1216]{2,1,0:T(8,128)(2,1)}, bf16[4,64,1216]{2,1,0:T(8,128)(2,1)}, u32[]{:S(2)}, u32[]{:S(2)}) %collective-permute-start.24) | collective-permute-done | bytes 622624 | tf_op jit(solution)/shard_map/ppermute | solution.py:81
  431.8 2.8 collective-permute-start.28
  434.6 3.2 collective-permute-done.26
  437.9 2.4 collective-permute-done.27
  440.4 2.4 collective-permute-start.32
  442.8 4.2 collective-permute-start.33
  451.9 3.2 collective-permute-start.35
  455.2 3.3 fusion.50
  460.0 7.7 %collective-permute-start.39 = (bf16[176,512]{1,0:T(8,128)(2,1)}, bf16[176,512]{1,0:T(8,128)(2,1)}, u32[]{:S(2)}, u32[]{:S(2)}) collective-permute-start(bf16[176,512]{1,0:T(8,128)(2,1)} %reduce-scatter.5.cloned.1.call-done), channel_id=1, source_target_pairs={{0,0},{1,32},{2,64},{3,96},{32,1},{33,33},{34,65},{35,97},{64,2},{... | collective-permute-start | bytes 540680 | tf_op jit(solution)/shard_map/ppermute | solution.py:111
  472.8 3.2 collective-permute-start.36
  476.0 8.4 %collective-permute-done.40.p1 = bf16[176,512]{1,0:T(8,128)(2,1)} collective-permute-done((bf16[176,512]{1,0:T(8,128)(2,1)}, bf16[176,512]{1,0:T(8,128)(2,1)}, u32[]{:S(2)}, u32[]{:S(2)}) %collective-permute-start.40) | collective-permute-done | bytes 180256 | tf_op jit(solution)/shard_map/ppermute | solution.py:111
  488.2 2.5 shard_map.305
  490.8 3.9 shard_map.308
  495.6 7.3 %shard_map.307 = (f32[64,11264]{1,0:T(8,128)}, f32[64,11264]{1,0:T(8,128)}, f32[64,11264]{1,0:T(8,128)}) custom-call(s32[1]{0:T(128)} %bitcast.38.place, bf16[64,2816]{1,0:T(8,128)(2,1)S(1)} %copy-done.10, bf16[64,2816]{1,0:T(8,128)(2,1)S(1)} %collective-permute-done.36.p1, bf16[64,2816]{1,0:T(8,128)(2,1)S(1)} %collective-permute-done.37.p2, ...), custom_call_target="tpu_custom_call" | custom-call | flops 8650752 | bytes 18743296 | tf_op jit(solution)/shard_map/pallas_call | solution.py:220
  (254 shorter events, 103.5 us)
Async XLA Ops:
  7.2 24.5 %copy-start.31 = (bf16[128,2048]{1,0:T(8,128)(2,1)S(1)}, bf16[128,2048]{1,0:T(8,128)(2,1)}, u32[]{:S(2)}) copy-start(bf16[128,2048]{1,0:T(8,128)(2,1)} %param.19) | copy-start | bytes 1572868
  7.2 24.7 %copy-start.11 = (bf16[128,2048]{1,0:T(8,128)(2,1)S(1)}, bf16[128,2048]{1,0:T(8,128)(2,1)}, u32[]{:S(2)}) copy-start(bf16[128,2048]{1,0:T(8,128)(2,1)} %param.18) | copy-start | bytes 1572868
  7.2 81.2 %all-gather.4.cloned.1.call-start = ((), (), s32[]{:S(2)}) async-start(), calls=%async_computation.2 | async-start | bytes 4866048 | tf_op jit(solution)/shard_map/all_gather | solution.py:69
  9.3 18.2 %collective-permute-start.3 = (bf16[240,512]{1,0:T(8,128)(2,1)S(1)}, bf16[240,512]{1,0:T(8,128)(2,1)S(1)}, u32[]{:S(2)}, u32[]{:S(2)}) collective-permute-start(bf16[240,512]{1,0:T(8,128)(2,1)S(1)} %pad_maximum_fusion.11), channel_id=1, source_target_pairs={{0,0},{1,32},{2,64},{3,96},{32,1},{33,33},{34,65},{35,97},{64,2},{... | collective-permute-start | bytes 737288 | tf_op jit(solution)/shard_map/ppermute | solution.py:65
  28.3 113.5 %all-gather.8.cloned.1.call-start = ((), (), s32[]{:S(2)}) async-start(), calls=%async_computation.4 | async-start | bytes 5947392 | tf_op jit(solution)/shard_map/all_gather | solution.py:69
  29.0 157.6 %all-gather.6.cloned.1.call-start = ((), (), s32[]{:S(2)}) async-start(), calls=%async_computation.3 | async-start | bytes 11894784 | tf_op jit(solution)/shard_map/all_gather | solution.py:69
  31.0 429.0 %reduce-scatter.5.cloned.1.call-start = ((), (), s32[]{:S(2)}) async-start(), calls=%async_computation.6 | async-start | bytes 5947392 | tf_op jit(solution)/shard_map/reduce_scatter | solution.py:98
  32.0 26.1 %collective-permute-start = (bf16[128,4096]{1,0:T(8,128)(2,1)S(1)}, bf16[128,4096]{1,0:T(8,128)(2,1)S(1)}, u32[]{:S(2)}, u32[]{:S(2)}) collective-permute-start(bf16[128,4096]{1,0:T(8,128)(2,1)S(1)} %pad_maximum_fusion.7), channel_id=1, source_target_pairs={{1,0},{2,1},{3,2},{0,3},{5,4},{6,5},{7,6},{4,7},{9,8},{10,9},{11,1... | collective-permute-start | bytes 3145736 | tf_op jit(solution)/shard_map/ppermute | solution.py:45
  32.1 27.7 %collective-permute-start.1 = (bf16[128,4096]{1,0:T(8,128)(2,1)S(1)}, bf16[128,4096]{1,0:T(8,128)(2,1)S(1)}, u32[]{:S(2)}, u32[]{:S(2)}) collective-permute-start(bf16[128,4096]{1,0:T(8,128)(2,1)S(1)} %pad_maximum_fusion.7), channel_id=1, source_target_pairs={{2,0},{3,1},{0,2},{1,3},{6,4},{7,5},{4,6},{5,7},{10,8},{11,9},{8,1... | collective-permute-start | bytes 3145736 | tf_op jit(solution)/shard_map/ppermute | solution.py:45
  32.4 48.7 %collective-permute-start.2 = (bf16[128,4096]{1,0:T(8,128)(2,1)S(1)}, bf16[128,4096]{1,0:T(8,128)(2,1)S(1)}, u32[]{:S(2)}, u32[]{:S(2)}) collective-permute-start(bf16[128,4096]{1,0:T(8,128)(2,1)S(1)} %pad_maximum_fusion.7), channel_id=1, source_target_pairs={{3,0},{0,1},{1,2},{2,3},{7,4},{4,5},{5,6},{6,7},{11,8},{8,9},{9,10... | collective-permute-start | bytes 3145736 | tf_op jit(solution)/shard_map/ppermute | solution.py:45
  58.1 28.2 %copy-start.13 = (bf16[128,4096]{1,0:T(8,128)(2,1)}, bf16[128,4096]{1,0:T(8,128)(2,1)S(1)}, u32[]{:S(2)}) copy-start(bf16[128,4096]{1,0:T(8,128)(2,1)S(1)} %collective-permute-done) | copy-start | bytes 3145732
  59.7 26.5 %copy-start.16 = (bf16[128,4096]{1,0:T(8,128)(2,1)}, bf16[128,4096]{1,0:T(8,128)(2,1)S(1)}, u32[]{:S(2)}) copy-start(bf16[128,4096]{1,0:T(8,128)(2,1)S(1)} %collective-permute-done.1) | copy-start | bytes 3145732
  88.4 308.9 %copy-start.43 = (f32[512]{0:T(512)}, f32[512]{0:T(512)S(1)}, u32[]{:S(2)}) copy-start(f32[512]{0:T(512)S(1)} %add_rsqrt_fusion) | copy-start | bytes 6148
  107.6 19.9 %collective-permute-start.4 = (bf16[128,2048]{1,0:T(8,128)(2,1)}, bf16[128,2048]{1,0:T(8,128)(2,1)}, u32[]{:S(2)}, u32[]{:S(2)}) collective-permute-start(bf16[128,2048]{1,0:T(8,128)(2,1)} %copy.73), channel_id=1, source_target_pairs={{0,2},{1,3},{2,0},{3,1},{4,6},{5,7},{6,4},{7,5},{8,10},{9,11},{10,... | collective-permute-start | bytes 1572872 | tf_op jit(solution)/shard_map/ppermute | solution.py:49
  109.9 24.5 %collective-permute-start.5 = (bf16[128,2048]{1,0:T(8,128)(2,1)}, bf16[128,2048]{1,0:T(8,128)(2,1)}, u32[]{:S(2)}, u32[]{:S(2)}) collective-permute-start(bf16[128,2048]{1,0:T(8,128)(2,1)} %copy.75), channel_id=1, source_target_pairs={{0,1},{1,2},{2,3},{3,0},{4,5},{5,6},{6,7},{7,4},{8,9},{9,10},{10,1... | collective-permute-start | bytes 1572872 | tf_op jit(solution)/shard_map/ppermute | solution.py:49
  113.9 20.6 %collective-permute-start.6 = (bf16[128,2048]{1,0:T(8,128)(2,1)}, bf16[128,2048]{1,0:T(8,128)(2,1)}, u32[]{:S(2)}, u32[]{:S(2)}) collective-permute-start(bf16[128,2048]{1,0:T(8,128)(2,1)} %copy.76), channel_id=1, source_target_pairs={{0,3},{1,0},{2,1},{3,2},{4,7},{5,4},{6,5},{7,6},{8,11},{9,8},{10,9... | collective-permute-start | bytes 1572872 | tf_op jit(solution)/shard_map/ppermute | solution.py:49
  139.7 15.1 %collective-permute-start.7 = (bf16[128,2048]{1,0:T(8,128)(2,1)}, bf16[128,2048]{1,0:T(8,128)(2,1)}, u32[]{:S(2)}, u32[]{:S(2)}) collective-permute-start(bf16[128,2048]{1,0:T(8,128)(2,1)} %multiply_convert_fusion.4), channel_id=1, source_target_pairs={{1,0},{2,1},{3,2},{0,3},{5,4},{6,5},{7,6},{4,7},{9,8},{10,9},{11,1... | collective-permute-start | bytes 1572872 | tf_op jit(solution)/shard_map/ppermute | solution.py:45
  140.3 16.7 %collective-permute-start.8 = (bf16[128,2048]{1,0:T(8,128)(2,1)}, bf16[128,2048]{1,0:T(8,128)(2,1)}, u32[]{:S(2)}, u32[]{:S(2)}) collective-permute-start(bf16[128,2048]{1,0:T(8,128)(2,1)} %multiply_convert_fusion.4), channel_id=1, source_target_pairs={{2,0},{3,1},{0,2},{1,3},{6,4},{7,5},{4,6},{5,7},{10,8},{11,9},{8,1... | collective-permute-start | bytes 1572872 | tf_op jit(solution)/shard_map/ppermute | solution.py:45
  140.7 26.0 %collective-permute-start.9 = (bf16[128,2048]{1,0:T(8,128)(2,1)}, bf16[128,2048]{1,0:T(8,128)(2,1)}, u32[]{:S(2)}, u32[]{:S(2)}) collective-permute-start(bf16[128,2048]{1,0:T(8,128)(2,1)} %multiply_convert_fusion.4), channel_id=1, source_target_pairs={{3,0},{0,1},{1,2},{2,3},{7,4},{4,5},{5,6},{6,7},{11,8},{8,9},{9,10... | collective-permute-start | bytes 1572872 | tf_op jit(solution)/shard_map/ppermute | solution.py:45
  186.6 10.3 %copy-start.29 = (f32[512,1408]{1,0:T(8,128)S(1)}, f32[512,1408]{1,0:T(8,128)}, u32[]{:S(2)}) copy-start(f32[512,1408]{1,0:T(8,128)} %fusion.32) | copy-start | bytes 8650756
  186.6 10.3 %copy-start.30 = (f32[512,1408]{1,0:T(8,128)S(1)}, f32[512,1408]{1,0:T(8,128)}, u32[]{:S(2)}) copy-start(f32[512,1408]{1,0:T(8,128)} %fusion.34) | copy-start | bytes 8650756
  219.6 253.2 %reduce-scatter.3.cloned.1.call-start = ((), (), s32[]{:S(2)}) async-start(), calls=%async_computation.5 | async-start | bytes 11894784 | tf_op jit(solution)/shard_map/reduce_scatter | solution.py:98
  253.3 27.4 %collective-permute-start.13 = (bf16[128,2048]{1,0:T(8,128)(2,1)}, bf16[128,2048]{1,0:T(8,128)(2,1)}, u32[]{:S(2)}, u32[]{:S(2)}) collective-permute-start(bf16[128,2048]{1,0:T(8,128)(2,1)} %get-tuple-element.64), channel_id=1, source_target_pairs={{0,2},{1,3},{2,0},{3,1},{4,6},{5,7},{6,4},{7,5},{8,10},{9,11},{10,... | collective-permute-start | bytes 1572872 | tf_op jit(solution)/shard_map/ppermute | solution.py:49
  256.3 26.8 %collective-permute-start.14 = (bf16[128,2048]{1,0:T(8,128)(2,1)}, bf16[128,2048]{1,0:T(8,128)(2,1)}, u32[]{:S(2)}, u32[]{:S(2)}) collective-permute-start(bf16[128,2048]{1,0:T(8,128)(2,1)} %get-tuple-element.66), channel_id=1, source_target_pairs={{0,1},{1,2},{2,3},{3,0},{4,5},{5,6},{6,7},{7,4},{8,9},{9,10},{10,1... | collective-permute-start | bytes 1572872 | tf_op jit(solution)/shard_map/ppermute | solution.py:49
  256.8 26.2 %collective-permute-start.15 = (bf16[128,2048]{1,0:T(8,128)(2,1)}, bf16[128,2048]{1,0:T(8,128)(2,1)}, u32[]{:S(2)}, u32[]{:S(2)}) collective-permute-start(bf16[128,2048]{1,0:T(8,128)(2,1)} %get-tuple-element.65), channel_id=1, source_target_pairs={{0,3},{1,0},{2,1},{3,2},{4,7},{5,4},{6,5},{7,6},{8,11},{9,8},{10,9... | collective-permute-start | bytes 1572872 | tf_op jit(solution)/shard_map/ppermute | solution.py:49
  271.8 20.6 %collective-permute-start.10 = (bf16[128,2048]{1,0:T(8,128)(2,1)}, bf16[128,2048]{1,0:T(8,128)(2,1)}, u32[]{:S(2)}, u32[]{:S(2)}) collective-permute-start(bf16[128,2048]{1,0:T(8,128)(2,1)} %copy.78), channel_id=1, source_target_pairs={{0,2},{1,3},{2,0},{3,1},{4,6},{5,7},{6,4},{7,5},{8,10},{9,11},{10,... | collective-permute-start | bytes 1572872 | tf_op jit(solution)/shard_map/ppermute | solution.py:49
  273.8 29.1 %collective-permute-start.11 = (bf16[128,2048]{1,0:T(8,128)(2,1)}, bf16[128,2048]{1,0:T(8,128)(2,1)}, u32[]{:S(2)}, u32[]{:S(2)}) collective-permute-start(bf16[128,2048]{1,0:T(8,128)(2,1)} %copy.80), channel_id=1, source_target_pairs={{0,1},{1,2},{2,3},{3,0},{4,5},{5,6},{6,7},{7,4},{8,9},{9,10},{10,1... | collective-permute-start | bytes 1572872 | tf_op jit(solution)/shard_map/ppermute | solution.py:49
  280.7 22.2 %copy-start.26 = (f32[128,2048]{1,0:T(8,128)S(1)}, f32[128,2048]{1,0:T(8,128)}, u32[]{:S(2)}) copy-start(f32[128,2048]{1,0:T(8,128)} %copy.79) | copy-start | bytes 3145732
  280.7 22.2 %copy-start.32 = (bf16[128,2048]{1,0:T(8,128)(2,1)S(1)}, bf16[128,2048]{1,0:T(8,128)(2,1)}, u32[]{:S(2)}) copy-start(bf16[128,2048]{1,0:T(8,128)(2,1)} %param.19) | copy-start | bytes 1572868
  280.7 22.2 %collective-permute-start.12 = (bf16[128,2048]{1,0:T(8,128)(2,1)S(1)}, bf16[128,2048]{1,0:T(8,128)(2,1)S(1)}, u32[]{:S(2)}, u32[]{:S(2)}) collective-permute-start(bf16[128,2048]{1,0:T(8,128)(2,1)S(1)} %copy-done.39), channel_id=1, source_target_pairs={{0,3},{1,0},{2,1},{3,2},{4,7},{5,4},{6,5},{7,6},{8,11},{9,8},{10,9... | collective-permute-start | bytes 1572872 | tf_op jit(solution)/shard_map/ppermute | solution.py:49
  306.6 25.5 %collective-permute-start.16 = (bf16[128,2048]{1,0:T(8,128)(2,1)}, bf16[128,2048]{1,0:T(8,128)(2,1)}, u32[]{:S(2)}, u32[]{:S(2)}) collective-permute-start(bf16[128,2048]{1,0:T(8,128)(2,1)} %get-tuple-element.46), channel_id=1, source_target_pairs={{1,0},{2,1},{3,2},{0,3},{5,4},{6,5},{7,6},{4,7},{9,8},{10,9},{11,1... | collective-permute-start | bytes 1572872 | tf_op jit(solution)/shard_map/ppermute | solution.py:45
  309.2 22.9 %collective-permute-start.17 = (bf16[128,2048]{1,0:T(8,128)(2,1)}, bf16[128,2048]{1,0:T(8,128)(2,1)}, u32[]{:S(2)}, u32[]{:S(2)}) collective-permute-start(bf16[128,2048]{1,0:T(8,128)(2,1)} %get-tuple-element.46), channel_id=1, source_target_pairs={{2,0},{3,1},{0,2},{1,3},{6,4},{7,5},{4,6},{5,7},{10,8},{11,9},{8,1... | collective-permute-start | bytes 1572872 | tf_op jit(solution)/shard_map/ppermute | solution.py:45
  310.2 25.6 %collective-permute-start.18 = (bf16[128,2048]{1,0:T(8,128)(2,1)}, bf16[128,2048]{1,0:T(8,128)(2,1)}, u32[]{:S(2)}, u32[]{:S(2)}) collective-permute-start(bf16[128,2048]{1,0:T(8,128)(2,1)} %get-tuple-element.46), channel_id=1, source_target_pairs={{3,0},{0,1},{1,2},{2,3},{7,4},{4,5},{5,6},{6,7},{11,8},{8,9},{9,10... | collective-permute-start | bytes 1572872 | tf_op jit(solution)/shard_map/ppermute | solution.py:45
  377.3 7.6 %collective-permute-start.22 = (bf16[4,4,64,1216]{3,2,1,0:T(8,128)(2,1)S(1)}, bf16[4,4,64,1216]{3,2,1,0:T(8,128)(2,1)}, u32[]{:S(2)}, u32[]{:S(2)}) collective-permute-start(bf16[4,4,64,1216]{3,2,1,0:T(8,128)(2,1)S(1)} %dynamic-slice_bitcast_fusion), channel_id=1, source_target_pairs={{0,4},{4,0},{1,5},{5,1},{2,6},{6,2},{3,7},{7,3},{8,12},{12,8},{9,1... | collective-permute-start | bytes 7471112 | tf_op jit(solution)/shard_map/ppermute | solution.py:90
  380.1 16.4 %collective-permute-start.19 = (bf16[128,2048]{1,0:T(8,128)(2,1)S(1)}, bf16[128,2048]{1,0:T(8,128)(2,1)}, u32[]{:S(2)}, u32[]{:S(2)}) collective-permute-start(bf16[128,2048]{1,0:T(8,128)(2,1)S(1)} %get-tuple-element.61), channel_id=1, source_target_pairs={{0,2},{1,3},{2,0},{3,1},{4,6},{5,7},{6,4},{7,5},{8,10},{9,11},{10,... | collective-permute-start | bytes 1572872 | tf_op jit(solution)/shard_map/ppermute | solution.py:49
  381.7 25.5 %collective-permute-start.20 = (bf16[128,2048]{1,0:T(8,128)(2,1)}, bf16[128,2048]{1,0:T(8,128)(2,1)}, u32[]{:S(2)}, u32[]{:S(2)}) collective-permute-start(bf16[128,2048]{1,0:T(8,128)(2,1)} %get-tuple-element.63), channel_id=1, source_target_pairs={{0,1},{1,2},{2,3},{3,0},{4,5},{5,6},{6,7},{7,4},{8,9},{9,10},{10,1... | collective-permute-start | bytes 1572872 | tf_op jit(solution)/shard_map/ppermute | solution.py:49
  382.0 25.2 %collective-permute-start.21 = (bf16[128,2048]{1,0:T(8,128)(2,1)}, bf16[128,2048]{1,0:T(8,128)(2,1)}, u32[]{:S(2)}, u32[]{:S(2)}) collective-permute-start(bf16[128,2048]{1,0:T(8,128)(2,1)} %get-tuple-element.62), channel_id=1, source_target_pairs={{0,3},{1,0},{2,1},{3,2},{4,7},{5,4},{6,5},{7,6},{8,11},{9,8},{10,9... | collective-permute-start | bytes 1572872 | tf_op jit(solution)/shard_map/ppermute | solution.py:49
  389.6 23.4 %collective-permute-start.23 = (bf16[4,64,1216]{2,1,0:T(8,128)(2,1)}, bf16[4,64,1216]{2,1,0:T(8,128)(2,1)}, u32[]{:S(2)}, u32[]{:S(2)}) collective-permute-start(bf16[4,64,1216]{2,1,0:T(8,128)(2,1)} %get-tuple-element.58), channel_id=1, source_target_pairs={{0,64},{32,96},{64,0},{96,32},{1,65},{33,97},{65,1},{97,33},{2,66}... | collective-permute-start | bytes 1867784 | tf_op jit(solution)/shard_map/ppermute | solution.py:81
  390.9 34.2 %collective-permute-start.24 = (bf16[4,64,1216]{2,1,0:T(8,128)(2,1)}, bf16[4,64,1216]{2,1,0:T(8,128)(2,1)}, u32[]{:S(2)}, u32[]{:S(2)}) collective-permute-start(bf16[4,64,1216]{2,1,0:T(8,128)(2,1)} %get-tuple-element.60), channel_id=1, source_target_pairs={{0,32},{32,64},{64,96},{96,0},{1,33},{33,65},{65,97},{97,1},{2,34}... | collective-permute-start | bytes 1867784 | tf_op jit(solution)/shard_map/ppermute | solution.py:81
  396.6 30.8 %collective-permute-start.25 = (bf16[4,64,1216]{2,1,0:T(8,128)(2,1)}, bf16[4,64,1216]{2,1,0:T(8,128)(2,1)}, u32[]{:S(2)}, u32[]{:S(2)}) collective-permute-start(bf16[4,64,1216]{2,1,0:T(8,128)(2,1)} %get-tuple-element.59), channel_id=1, source_target_pairs={{0,96},{32,0},{64,32},{96,64},{1,97},{33,1},{65,33},{97,65},{2,98}... | collective-permute-start | bytes 1867784 | tf_op jit(solution)/shard_map/ppermute | solution.py:81
  409.3 45.8 %copy-start.27 = (f32[128,2048]{1,0:T(8,128)S(1)}, f32[128,2048]{1,0:T(8,128)}, u32[]{:S(2)}) copy-start(f32[128,2048]{1,0:T(8,128)} %get-tuple-element.47) | copy-start | bytes 3145732
  409.3 45.8 %slice-start.1 = ((f32[512]{0:T(512)}), f32[128]{0:T(128)S(1)}, s32[]{:S(2)}) async-start(f32[512]{0:T(512)} %copy-done.43), calls=%async_computation.8 | async-start | bytes 1024 | tf_op jit(solution)/shard_map/slice | solution.py:366
  429.2 8.7 %collective-permute-start.26 = (bf16[64,1216]{1,0:T(8,128)(2,1)S(1)}, bf16[64,1216]{1,0:T(8,128)(2,1)S(1)}, u32[]{:S(2)}, u32[]{:S(2)}) collective-permute-start(bf16[64,1216]{1,0:T(8,128)(2,1)S(1)} %get-tuple-element.78), channel_id=1, source_target_pairs={{0,16},{8,24},{16,0},{24,8},{1,17},{9,25},{17,1},{25,9},{2,18},{10... | collective-permute-start | bytes 466952 | tf_op jit(solution)/shard_map/ppermute | solution.py:81
  431.4 8.9 %collective-permute-start.27 = (bf16[64,1216]{1,0:T(8,128)(2,1)S(1)}, bf16[64,1216]{1,0:T(8,128)(2,1)S(1)}, u32[]{:S(2)}, u32[]{:S(2)}) collective-permute-start(bf16[64,1216]{1,0:T(8,128)(2,1)S(1)} %get-tuple-element.80), channel_id=1, source_target_pairs={{0,8},{8,16},{16,24},{24,0},{1,9},{9,17},{17,25},{25,1},{2,10},{10... | collective-permute-start | bytes 466952 | tf_op jit(solution)/shard_map/ppermute | solution.py:81
  431.8 8.4 %collective-permute-start.28 = (bf16[64,1216]{1,0:T(8,128)(2,1)S(1)}, bf16[64,1216]{1,0:T(8,128)(2,1)S(1)}, u32[]{:S(2)}, u32[]{:S(2)}) collective-permute-start(bf16[64,1216]{1,0:T(8,128)(2,1)S(1)} %get-tuple-element.79), channel_id=1, source_target_pairs={{0,24},{8,0},{16,8},{24,16},{1,25},{9,1},{17,9},{25,17},{2,26},{10... | collective-permute-start | bytes 466952 | tf_op jit(solution)/shard_map/ppermute | solution.py:81
  440.4 18.1 %copy-start.37 = (bf16[64,1216]{1,0:T(8,128)(2,1)}, bf16[64,1216]{1,0:T(8,128)(2,1)S(1)}, u32[]{:S(2)}) copy-start(bf16[64,1216]{1,0:T(8,128)(2,1)S(1)} %fusion.123) | copy-start | bytes 466948
  440.4 9.9 %collective-permute-start.32 = (bf16[64,512]{1,0:T(8,128)(2,1)S(1)}, bf16[64,512]{1,0:T(8,128)(2,1)S(1)}, u32[]{:S(2)}, u32[]{:S(2)}) collective-permute-start(bf16[64,512]{1,0:T(8,128)(2,1)S(1)} %slice.343), channel_id=1, source_target_pairs={{0,0},{1,32},{2,64},{3,96},{32,1},{33,33},{34,65},{35,97},{64,2},{... | collective-permute-start | bytes 196616 | tf_op jit(solution)/shard_map/ppermute | solution.py:111
  442.8 9.1 %collective-permute-start.33 = (bf16[64,512]{1,0:T(8,128)(2,1)S(1)}, bf16[64,512]{1,0:T(8,128)(2,1)S(1)}, u32[]{:S(2)}, u32[]{:S(2)}) collective-permute-start(bf16[64,512]{1,0:T(8,128)(2,1)S(1)} %slice.343), channel_id=1, source_target_pairs={{0,3},{1,35},{2,67},{3,99},{32,0},{33,32},{34,64},{35,96},{64,1},{... | collective-permute-start | bytes 196616 | tf_op jit(solution)/shard_map/ppermute | solution.py:111
  447.6 21.6 %collective-permute-start.29 = (bf16[64,704]{1,0:T(8,128)(2,1)}, bf16[64,704]{1,0:T(8,128)(2,1)}, u32[]{:S(2)}, u32[]{:S(2)}) collective-permute-start(bf16[64,704]{1,0:T(8,128)(2,1)} %pad_maximum_fusion.12.p0), channel_id=1, source_target_pairs={{1,0},{2,1},{3,2},{0,3},{5,4},{6,5},{7,6},{4,7},{9,8},{10,9},{11,1... | collective-permute-start | bytes 270344 | tf_op jit(solution)/shard_map/ppermute | solution.py:45
  447.6 21.6 %collective-permute-start.30 = (bf16[64,704]{1,0:T(8,128)(2,1)}, bf16[64,704]{1,0:T(8,128)(2,1)}, u32[]{:S(2)}, u32[]{:S(2)}) collective-permute-start(bf16[64,704]{1,0:T(8,128)(2,1)} %pad_maximum_fusion.12.p0), channel_id=1, source_target_pairs={{2,0},{3,1},{0,2},{1,3},{6,4},{7,5},{4,6},{5,7},{10,8},{11,9},{8,1... | collective-permute-start | bytes 270344 | tf_op jit(solution)/shard_map/ppermute | solution.py:45
  447.6 21.6 %collective-permute-start.31 = (bf16[64,704]{1,0:T(8,128)(2,1)}, bf16[64,704]{1,0:T(8,128)(2,1)}, u32[]{:S(2)}, u32[]{:S(2)}) collective-permute-start(bf16[64,704]{1,0:T(8,128)(2,1)} %pad_maximum_fusion.12.p0), channel_id=1, source_target_pairs={{3,0},{0,1},{1,2},{2,3},{7,4},{4,5},{5,6},{6,7},{11,8},{8,9},{9,10... | collective-permute-start | bytes 270344 | tf_op jit(solution)/shard_map/ppermute | solution.py:45
  450.3 8.3 %collective-permute-start.34 = (bf16[64,512]{1,0:T(8,128)(2,1)S(1)}, bf16[64,512]{1,0:T(8,128)(2,1)S(1)}, u32[]{:S(2)}, u32[]{:S(2)}) collective-permute-start(bf16[64,512]{1,0:T(8,128)(2,1)S(1)} %slice.343), channel_id=1, source_target_pairs={{0,2},{1,34},{2,66},{3,98},{32,3},{33,35},{34,67},{35,99},{64,0},{... | collective-permute-start | bytes 196616 | tf_op jit(solution)/shard_map/ppermute | solution.py:111
  451.9 6.7 %collective-permute-start.35 = (bf16[64,512]{1,0:T(8,128)(2,1)S(1)}, bf16[64,512]{1,0:T(8,128)(2,1)S(1)}, u32[]{:S(2)}, u32[]{:S(2)}) collective-permute-start(bf16[64,512]{1,0:T(8,128)(2,1)S(1)} %slice.343), channel_id=1, source_target_pairs={{0,1},{1,33},{2,65},{3,97},{32,2},{33,34},{34,66},{35,98},{64,3},{... | collective-permute-start | bytes 196616 | tf_op jit(solution)/shard_map/ppermute | solution.py:111
  455.2 30.9 %copy-start.4 = (f32[64,2560]{1,0:T(8,128)S(1)}, f32[64,2560]{1,0:T(8,128)}, u32[]{:S(2)}) copy-start(f32[64,2560]{1,0:T(8,128)} %weight.4) | copy-start | bytes 1966084
  458.5 32.3 %copy-start.1 = (f32[176,2048]{1,0:T(8,128)S(1)}, f32[176,2048]{1,0:T(8,128)}, u32[]{:S(2)}) copy-start(f32[176,2048]{1,0:T(8,128)} %weight.7) | copy-start | bytes 4325380
  458.5 32.3 %copy-start.2 = (f32[176,2048]{1,0:T(8,128)S(1)}, f32[176,2048]{1,0:T(8,128)}, u32[]{:S(2)}) copy-start(f32[176,2048]{1,0:T(8,128)} %moment.7) | copy-start | bytes 4325380
  460.0 16.0 %collective-permute-start.39 = (bf16[176,512]{1,0:T(8,128)(2,1)}, bf16[176,512]{1,0:T(8,128)(2,1)}, u32[]{:S(2)}, u32[]{:S(2)}) collective-permute-start(bf16[176,512]{1,0:T(8,128)(2,1)} %reduce-scatter.5.cloned.1.call-done), channel_id=1, source_target_pairs={{0,0},{1,32},{2,64},{3,96},{32,1},{33,33},{34,65},{35,97},{64,2},{... | collective-permute-start | bytes 540680 | tf_op jit(solution)/shard_map/ppermute | solution.py:111
  467.7 16.7 %collective-permute-start.40 = (bf16[176,512]{1,0:T(8,128)(2,1)}, bf16[176,512]{1,0:T(8,128)(2,1)}, u32[]{:S(2)}, u32[]{:S(2)}) collective-permute-start(bf16[176,512]{1,0:T(8,128)(2,1)} %reduce-scatter.5.cloned.1.call-done), channel_id=1, source_target_pairs={{0,3},{1,35},{2,67},{3,99},{32,0},{33,32},{34,64},{35,96},{64,1},{... | collective-permute-start | bytes 540680 | tf_op jit(solution)/shard_map/ppermute | solution.py:111
  471.5 19.3 %collective-permute-start.41 = (bf16[176,512]{1,0:T(8,128)(2,1)}, bf16[176,512]{1,0:T(8,128)(2,1)}, u32[]{:S(2)}, u32[]{:S(2)}) collective-permute-start(bf16[176,512]{1,0:T(8,128)(2,1)} %reduce-scatter.5.cloned.1.call-done), channel_id=1, source_target_pairs={{0,2},{1,34},{2,66},{3,98},{32,3},{33,35},{34,67},{35,99},{64,0},{... | collective-permute-start | bytes 540680 | tf_op jit(solution)/shard_map/ppermute | solution.py:111
  472.8 18.0 %collective-permute-start.42 = (bf16[176,512]{1,0:T(8,128)(2,1)}, bf16[176,512]{1,0:T(8,128)(2,1)}, u32[]{:S(2)}, u32[]{:S(2)}) collective-permute-start(bf16[176,512]{1,0:T(8,128)(2,1)} %reduce-scatter.5.cloned.1.call-done), channel_id=1, source_target_pairs={{0,1},{1,33},{2,65},{3,97},{32,2},{33,34},{34,66},{35,98},{64,3},{... | collective-permute-start | bytes 540680 | tf_op jit(solution)/shard_map/ppermute | solution.py:111
  472.8 18.0 %copy-start.3 = (f32[176,2048]{1,0:T(8,128)S(1)}, f32[176,2048]{1,0:T(8,128)}, u32[]{:S(2)}) copy-start(f32[176,2048]{1,0:T(8,128)} %second.7) | copy-start | bytes 4325380
  472.8 21.9 %collective-permute-start.36 = (bf16[64,2816]{1,0:T(8,128)(2,1)}, bf16[64,2816]{1,0:T(8,128)(2,1)S(1)}, u32[]{:S(2)}, u32[]{:S(2)}) collective-permute-start(bf16[64,2816]{1,0:T(8,128)(2,1)} %reduce-scatter.3.cloned.1.call-done.p0), channel_id=1, source_target_pairs={{1,0},{2,1},{3,2},{0,3},{5,4},{6,5},{7,6},{4,7},{9,8},{10,9},{11,1... | collective-permute-start | bytes 1081352 | tf_op jit(solution)/shard_map/ppermute | solution.py:45
  476.0 18.7 %collective-permute-start.37 = (bf16[64,2816]{1,0:T(8,128)(2,1)}, bf16[64,2816]{1,0:T(8,128)(2,1)S(1)}, u32[]{:S(2)}, u32[]{:S(2)}) collective-permute-start(bf16[64,2816]{1,0:T(8,128)(2,1)} %reduce-scatter.3.cloned.1.call-done.p0), channel_id=1, source_target_pairs={{2,0},{3,1},{0,2},{1,3},{6,4},{7,5},{4,6},{5,7},{10,8},{11,9},{8,1... | collective-permute-start | bytes 1081352 | tf_op jit(solution)/shard_map/ppermute | solution.py:45
  484.4 11.1 %collective-permute-start.38 = (bf16[64,2816]{1,0:T(8,128)(2,1)}, bf16[64,2816]{1,0:T(8,128)(2,1)S(1)}, u32[]{:S(2)}, u32[]{:S(2)}) collective-permute-start(bf16[64,2816]{1,0:T(8,128)(2,1)} %reduce-scatter.3.cloned.1.call-done.p0), channel_id=1, source_target_pairs={{3,0},{0,1},{1,2},{2,3},{7,4},{4,5},{5,6},{6,7},{11,8},{8,9},{9,10... | collective-permute-start | bytes 1081352 | tf_op jit(solution)/shard_map/ppermute | solution.py:45
  (32 other events, 159.2 us)
Sparse Core Ops, SparseCore 0:
  28.4 45.2 all-gather.3
  76.5 47.4 all-gather.7
  126.8 59.7 all-gather.5
  219.8 84.8 reduce-scatter.4
  308.7 111.1 reduce-scatter.2
